TPU v7x, 128 devices: a whole 4x4x4 slice. The times are simulated.
128 devices in a mesh: row: 16 (over x, y_lo, core), col: 8 (over y_hi, z).
Axes of the slice: x: 4, y: 4 (y_hi: 2, y_lo: 2; y = y_hi * 2 + y_lo), z: 4, core: 2. Of those that a mesh axis runs over, the one named last changes fastest.
Arguments:
- front: float32 [16384, 16384], P('row', 'col'), may hold values from -0.03 to 5, as said below
- children: float32 [2, 6144, 6144], P(None, 'row', 'col'), may hold values from -0.02 to 1, as said below
- child_map: int32 [2, 48], replicated, may hold values from 0 to 127, as said below
Outputs:
- front_out: float32 [16384, 16384], P('row', 'col')
- lower_panel: float32 [16384, 1024], P('row')
Inputs may be any that keep to these rules, and one draw needn't show every extreme that they name: Each row of child_map is strictly increasing; each aligned run of 16 child tiles maps to 16 consecutive parent tiles. `front`: symmetric in natural order, and the assembled front is positive definite. `children`: each block is symmetric in natural order.
All inputs are finite; a program needn't handle non-finite values.
Results may differ from a plain program's by a relative error of at most 0.0001.
Values sent between devices are 32-bit elements; how exact they have to be, the bound alone decides.
A program may use at most 128 MiB of HBM per device.

v0:
```python
import jax
import jax.numpy as jnp
from jax import lax
from jax.sharding import PartitionSpec as P

TILE = 128
RUN = 16
PANEL = 512
PIVOTS = 1024


HIGHEST = lax.Precision.HIGHEST


def passed_along(block, axis, distance):
    devices = range(lax.axis_size(axis))
    route = [((i - distance) % len(devices), i) for i in devices]
    return lax.ppermute(block, axis, route)


def from_root(shard, axis, root):
    mine = lax.axis_index(axis) == root
    return lax.psum(jnp.where(mine, shard, jnp.zeros_like(shard)), axis)


def panel_factor(matrix, panel_width):
    matrix_order = matrix.shape[0]
    working = matrix
    factor = jnp.zeros_like(matrix)
    for first_col in range(0, matrix_order, panel_width):
        after_col = first_col + panel_width
        diagonal_factor = jnp.linalg.cholesky(working[first_col:after_col, first_col:after_col])
        factor = factor.at[first_col:after_col, first_col:after_col].set(diagonal_factor)
        if after_col < matrix_order:
            below_rows = jax.scipy.linalg.solve_triangular(
                diagonal_factor, working[after_col:, first_col:after_col].T, lower=True
            ).T
            factor = factor.at[after_col:, first_col:after_col].set(below_rows)
            working = working.at[after_col:, after_col:].add(
                -jnp.dot(below_rows, below_rows.T, precision=HIGHEST)
            )
    return factor


def run_starts(child_map, devices):
    return jnp.repeat(child_map[:, ::RUN], RUN // devices, axis=1)


def relay_rows(blocks, starts):
    devices = lax.axis_size("row")
    amounts = starts % devices
    relayed = blocks
    for bit_index in range(devices.bit_length() - 1):
        shifted = passed_along(relayed, "row", 2**bit_index)
        chosen = amounts // 2**bit_index % 2 == 1
        relayed = jnp.where(chosen[:, :, None, None, None], shifted, relayed)
    return relayed


def relay_columns(blocks, starts):
    devices = lax.axis_size("col")
    amounts = starts % devices
    relayed = blocks
    for bit_index in range(devices.bit_length() - 1):
        shifted = passed_along(relayed, "col", 2**bit_index)
        chosen = amounts // 2**bit_index % 2 == 1
        relayed = jnp.where(chosen[:, None, None, :, None], shifted, relayed)
    return relayed


def parent_select(starts, devices, device_index, parent_tiles):
    local_offset = jnp.arange(starts.shape[1], dtype=jnp.int32) % (RUN // devices)
    source = (device_index - starts) % devices
    parent_slot = (starts + local_offset[None, :] * devices + source) // devices
    targets = jnp.arange(parent_tiles, dtype=jnp.int32)
    return (parent_slot[:, :, None] == targets[None, None, :]).astype(jnp.float32)


def per_device(front, children, child_map):
    row_devices = lax.axis_size("row")
    col_devices = lax.axis_size("col")
    row_index = lax.axis_index("row")
    col_index = lax.axis_index("col")
    local_rows, local_cols = front.shape
    child_rows = children.shape[1]
    child_cols = children.shape[2]
    blocks = children.reshape(2, child_rows // TILE, TILE, child_cols // TILE, TILE)
    row_starts = run_starts(child_map, row_devices)
    col_starts = run_starts(child_map, col_devices)
    move_rows, move_columns = (relay_rows, relay_columns)
    relayed = move_columns(move_rows(blocks, row_starts), col_starts)
    row_select = parent_select(row_starts, row_devices, row_index, local_rows // TILE)
    col_select = parent_select(col_starts, col_devices, col_index, local_cols // TILE)
    lifted = jnp.einsum("ckl,ckamb->clamb", row_select, relayed, precision=HIGHEST)
    placed = jnp.einsum("clamb,cmn->lanb", lifted, col_select, precision=HIGHEST)
    assembled = front + placed.reshape(local_rows, local_cols)
    pivot_tiles = PIVOTS // TILE
    kept_tiles = pivot_tiles // col_devices
    pivot_strip = assembled[:, : kept_tiles * TILE]
    gathered = lax.all_gather(pivot_strip, "col", axis=1, tiled=True)
    pivot_columns = (
        gathered.reshape(local_rows, col_devices, kept_tiles, TILE)
        .transpose(0, 2, 1, 3)
        .reshape(local_rows, PIVOTS)
    )
    leading = pivot_columns[:TILE]
    stacked = lax.all_gather(leading, "row", axis=0, tiled=True)
    pivot_block = stacked[:PIVOTS]
    pivot_factor = panel_factor(pivot_block, PANEL)
    inverse = jax.scipy.linalg.solve_triangular(
        pivot_factor, jnp.eye(PIVOTS, dtype=jnp.float32), lower=True
    )
    solved = jnp.dot(pivot_columns, inverse.T, precision=HIGHEST)
    tile_number = jnp.arange(local_rows, dtype=jnp.int32) // TILE * row_devices + row_index
    in_pivot = tile_number < pivot_tiles
    own_factor = lax.dynamic_slice_in_dim(
        pivot_factor, jnp.minimum(row_index, pivot_tiles - 1) * TILE, TILE, 0
    )
    padded_factor = jnp.concatenate(
        [own_factor, jnp.zeros((local_rows - TILE, PIVOTS), jnp.float32)], axis=0
    )
    lower_panel = jnp.where(in_pivot[:, None], padded_factor, solved)
    update_rows = jnp.where(in_pivot[:, None], 0.0, solved)
    root_count = row_devices // col_devices
    received = []
    for root_step in range(root_count):
        arrived = from_root(update_rows, "row", col_index + col_devices * root_step)
        received.append(arrived.reshape(local_rows // TILE, TILE, PIVOTS))
    column_rows = jnp.stack(received, axis=1).reshape(local_cols, PIVOTS)
    front_out = assembled - jnp.einsum("ik,jk->ij", update_rows, column_rows, precision=HIGHEST)
    return (front_out, lower_panel)


def solution(mesh):
    placed = (P("row", "col"), P(None, "row", "col"), P())
    return jax.shard_map(
        per_device,
        mesh=mesh,
        in_specs=placed,
        out_specs=(P("row", "col"), P("row", None)),
        check_vma=False,
    )
```

profile of v0, /device:TPU:7, one launch (start us, length us, event | category | flops | bytes accessed | tf_op | source)
XLA Modules:
  0.0 1212.3 jit_solution(4116271432964249114)
XLA Ops:
  13.6 26.0 %collective-permute-done = f32[2,3,128,6,128]{4,2,3,1,0:T(8,128)} collective-permute-done((f32[2,3,128,6,128]{4,2,3,1,0:T(8,128)}, f32[2,3,128,6,128]{4,2,3,1,0:T(8,128)}, u32[]{:S(2)}, u32[]{:S(2)}) %collective-permute-start) | collective-permute-done | bytes 2359328 | tf_op jit(solution)/shard_map/ppermute | solution.py:18
  43.2 51.4 %collective-permute-done.1 = f32[2,3,128,6,128]{4,2,3,1,0:T(8,128)S(1)} collective-permute-done((f32[2,3,128,6,128]{4,2,3,1,0:T(8,128)S(1)}, f32[2,3,128,6,128]{4,2,3,1,0:T(8,128)S(1)}, u32[]{:S(2)}, u32[]{:S(2)}) %collective-permute-start.1) | collective-permute-done | bytes 2359328 | tf_op jit(solution)/shard_map/ppermute | solution.py:18
  96.9 49.3 %collective-permute-done.2 = f32[2,3,128,6,128]{4,2,3,1,0:T(8,128)S(1)} collective-permute-done((f32[2,3,128,6,128]{4,2,3,1,0:T(8,128)S(1)}, f32[2,3,128,6,128]{4,2,3,1,0:T(8,128)S(1)}, u32[]{:S(2)}, u32[]{:S(2)}) %collective-permute-start.2) | collective-permute-done | bytes 2359328 | tf_op jit(solution)/shard_map/ppermute | solution.py:18
  149.3 49.1 %collective-permute-done.3 = f32[2,3,128,6,128]{4,2,3,1,0:T(8,128)S(1)} collective-permute-done((f32[2,3,128,6,128]{4,2,3,1,0:T(8,128)S(1)}, f32[2,3,128,6,128]{4,2,3,1,0:T(8,128)S(1)}, u32[]{:S(2)}, u32[]{:S(2)}) %collective-permute-start.3) | collective-permute-done | bytes 2359328 | tf_op jit(solution)/shard_map/ppermute | solution.py:18
  203.9 50.0 %collective-permute-done.4 = f32[2,3,128,6,128]{4,2,3,1,0:T(8,128)} collective-permute-done((f32[2,3,128,6,128]{4,2,3,1,0:T(8,128)}, f32[2,3,128,6,128]{4,2,3,1,0:T(8,128)}, u32[]{:S(2)}, u32[]{:S(2)}) %collective-permute-start.4) | collective-permute-done | bytes 2359328 | tf_op jit(solution)/shard_map/ppermute | solution.py:18
  257.5 50.7 %collective-permute-done.5 = f32[2,3,128,6,128]{4,2,3,1,0:T(8,128)S(1)} collective-permute-done((f32[2,3,128,6,128]{4,2,3,1,0:T(8,128)S(1)}, f32[2,3,128,6,128]{4,2,3,1,0:T(8,128)S(1)}, u32[]{:S(2)}, u32[]{:S(2)}) %collective-permute-start.5) | collective-permute-done | bytes 2359328 | tf_op jit(solution)/shard_map/ppermute | solution.py:18
  321.9 36.3 %collective-permute-done.6 = f32[2,3,128,6,128]{4,2,3,1,0:T(8,128)} collective-permute-done((f32[2,3,128,6,128]{4,2,3,1,0:T(8,128)}, f32[2,3,128,6,128]{4,2,3,1,0:T(8,128)}, u32[]{:S(2)}, u32[]{:S(2)}) %collective-permute-start.6) | collective-permute-done | bytes 2359328 | tf_op jit(solution)/shard_map/ppermute | solution.py:18
  390.9 12.1 %add.233 = f32[1024,2048]{0,1:T(8,128)} add(f32[1024,2048]{0,1:T(8,128)} %copy.46, f32[1024,2048]{0,1:T(8,128)} %copy.64) | non-fusion elementwise | flops 2097152 | bytes 25165824 | tf_op jit(solution)/shard_map/add | solution.py:96
  405.0 80.7 %all-gather.3.cloned.1.call-done = f32[1024,1024]{0,1:T(8,128)} async-done(((f32[1024,128]{0,1:T(8,128)}), f32[1024,1024]{0,1:T(8,128)}) %all-gather.3.cloned.1.call-update) | async-done | bytes 4194320 | tf_op jit(solution)/shard_map/all_gather | solution.py:100
  491.7 54.0 %all-gather.5.cloned.1.call-done = f32[2048,1024]{0,1:T(8,128)} async-done(((f32[128,1024]{0,1:T(8,128)}), f32[2048,1024]{0,1:T(8,128)}) %all-gather.5.cloned.1.call-update) | async-done | bytes 8388624 | tf_op jit(solution)/shard_map/all_gather | solution.py:107
  549.2 11.7 cholesky.286
  571.5 11.7 cholesky.305
  594.2 11.7 cholesky.326
  617.0 11.9 cholesky.343
  634.2 14.1 %while.6 = (s32[]{:T(128)}, f32[512,512]{1,0:T(8,128)}, s32[4,2]{0,1:T(2,128)S(1)}, f32[4,128,128]{2,1,0:T(8,128)}, s32[]{:T(128)}) while((s32[]{:T(128)}, f32[512,512]{1,0:T(8,128)}, s32[4,2]{0,1:T(2,128)S(1)}, f32[4,128,128]{2,1,0:T(8,128)}, s32[]{:T(128)}) %tuple.104), condition=%wide.while_cond.4, body=%wide.while_body.4.sunk | while | flops 2 | bytes 132205 | solution.py:35
  648.3 40.1 %custom-call.28 = f32[4,128,128]{1,2,0:T(8,128)S(1)} custom-call(f32[4,128,128]{2,1,0:T(8,128)} %get-tuple-element.58), custom_call_target="InvertDiagBlocksLowerTriangular" | custom-call | tf_op jit(solution)/shard_map/jit(_solve_triangular)/triangular_solve | solution.py:35
  702.8 11.7 cholesky.358
  727.8 11.7 cholesky.377
  751.7 11.7 cholesky.398
  801.2 28.6 %while.7 = (s32[]{:T(128)}, f32[1024,1024]{1,0:T(8,128)}, s32[8,2]{0,1:T(2,128)S(1)}, f32[8,128,128]{2,1,0:T(8,128)}, s32[]{:T(128)}) while((s32[]{:T(128)}, f32[1024,1024]{1,0:T(8,128)}, s32[8,2]{0,1:T(2,128)S(1)}, f32[8,128,128]{2,1,0:T(8,128)}, s32[]{:T(128)}) %tuple.107), condition=%wide.while_cond.5, body=%wide.while_body.5.sunk | while | flops 2 | bytes 132205 | solution.py:110
  829.9 79.6 %custom-call.29 = f32[8,128,128]{1,2,0:T(8,128)S(1)} custom-call(f32[8,128,128]{2,1,0:T(8,128)} %get-tuple-element.66), custom_call_target="InvertDiagBlocksLowerTriangular" | custom-call | tf_op jit(solution)/shard_map/jit(_solve_triangular)/triangular_solve | solution.py:110
  932.7 30.6 %pad_select_fusion = (f32[1024,1024]{1,0:T(8,128)}, f32[1024,1024]{1,0:T(8,128)}, f32[1024,1024]{1,0:T(8,128)}, f32[1024,1024]{1,0:T(8,128)}) fusion(f32[128,1024]{1,0:T(8,128)S(1)} %constant_dynamic-slice_fusion.2, pred[1024]{0:T(1024)(128)(4,1)S(1)} %fusion.93, pred[]{:T(512)S(6)} %eq.114, pred[]{:T(512)S(6)} %eq.113, f32[1024,1024]{0,1:T(8,128)S(1)} %copy-done, ...), kind=kOutput, calls=%fused_computation.8 | convolution fusion | flops 12889096192 | bytes 25691138 | tf_op jit(solution)/shard_map/dot_general | solution.py:113
  963.3 196.6 %all-reduce.6.cloned.1.call-done = (f32[8,1,128,1024]{3,2,1,0:T(8,128)}, f32[8,1,128,1024]{3,2,1,0:T(8,128)}) async-done(((f32[8,1,128,1024]{3,2,1,0:T(8,128)}, f32[8,1,128,1024]{3,2,1,0:T(8,128)}), (f32[8,1,128,1024]{3,2,1,0:T(8,128)}, f32[8,1,128,1024]{3,2,1,0:T(8,128)})) %all-reduce.6.cloned.1.call-update) | async-done | bytes 8388624 | tf_op jit(solution)/shard_map/psum | solution.py:23
  1164.6 31.6 %convolution_subtract_fusion = f32[1024,2048]{0,1:T(8,128)} fusion(f32[1024,2048]{0,1:T(8,128)} %add.233, f32[2048,1024]{1,0:T(8,128)S(1)} %bitcast.166, f32[1024,1024]{1,0:T(8,128)S(1)} %copy-done.1, pred[1024]{0:T(1024)(128)(4,1)S(1)} %fusion.93), kind=kOutput, calls=%fused_computation.12 | convolution fusion | flops 25772949504 | bytes 29361152 | tf_op jit(solution)/shard_map/ik,jk->ij/dot_general | solution.py:130
  (193 shorter events, 272.1 us)
Async XLA Ops:
  7.2 478.6 %all-gather.3.cloned.1.call-start = ((), (), s32[]{:S(2)}) async-start(), calls=%async_computation | async-start | bytes 4718592 | tf_op jit(solution)/shard_map/all_gather | solution.py:100
  9.7 3.7 copy-start.10
  11.6 28.0 %collective-permute-start = (f32[2,3,128,6,128]{4,2,3,1,0:T(8,128)}, f32[2,3,128,6,128]{4,2,3,1,0:T(8,128)}, u32[]{:S(2)}, u32[]{:S(2)}) collective-permute-start(f32[2,3,128,6,128]{4,2,3,1,0:T(8,128)} %copy.29), channel_id=1, source_target_pairs={{120,0},{0,8},{8,16},{16,24},{24,32},{32,40},{40,48},{48,56},{56,6... | collective-permute-start | bytes 7077896 | tf_op jit(solution)/shard_map/ppermute | solution.py:18
  43.1 51.5 %collective-permute-start.1 = (f32[2,3,128,6,128]{4,2,3,1,0:T(8,128)S(1)}, f32[2,3,128,6,128]{4,2,3,1,0:T(8,128)S(1)}, u32[]{:S(2)}, u32[]{:S(2)}) collective-permute-start(f32[2,3,128,6,128]{4,2,3,1,0:T(8,128)S(1)} %copy.31), channel_id=1, source_target_pairs={{112,0},{120,8},{0,16},{8,24},{16,32},{24,40},{32,48},{40,56},{48,... | collective-permute-start | bytes 7077896 | tf_op jit(solution)/shard_map/ppermute | solution.py:18
  96.5 49.7 %collective-permute-start.2 = (f32[2,3,128,6,128]{4,2,3,1,0:T(8,128)S(1)}, f32[2,3,128,6,128]{4,2,3,1,0:T(8,128)S(1)}, u32[]{:S(2)}, u32[]{:S(2)}) collective-permute-start(f32[2,3,128,6,128]{4,2,3,1,0:T(8,128)S(1)} %copy.33), channel_id=1, source_target_pairs={{96,0},{104,8},{112,16},{120,24},{0,32},{8,40},{16,48},{24,56},{32... | collective-permute-start | bytes 7077896 | tf_op jit(solution)/shard_map/ppermute | solution.py:18
  148.1 50.3 %collective-permute-start.3 = (f32[2,3,128,6,128]{4,2,3,1,0:T(8,128)S(1)}, f32[2,3,128,6,128]{4,2,3,1,0:T(8,128)S(1)}, u32[]{:S(2)}, u32[]{:S(2)}) collective-permute-start(f32[2,3,128,6,128]{4,2,3,1,0:T(8,128)S(1)} %copy.35), channel_id=1, source_target_pairs={{64,0},{72,8},{80,16},{88,24},{96,32},{104,40},{112,48},{120,56},{... | collective-permute-start | bytes 7077896 | tf_op jit(solution)/shard_map/ppermute | solution.py:18
  201.7 52.1 %collective-permute-start.4 = (f32[2,3,128,6,128]{4,2,3,1,0:T(8,128)}, f32[2,3,128,6,128]{4,2,3,1,0:T(8,128)}, u32[]{:S(2)}, u32[]{:S(2)}) collective-permute-start(f32[2,3,128,6,128]{4,2,3,1,0:T(8,128)} %copy.37), channel_id=1, source_target_pairs={{7,0},{0,1},{1,2},{2,3},{3,4},{4,5},{5,6},{6,7},{15,8},{8,9},{9,10... | collective-permute-start | bytes 7077896 | tf_op jit(solution)/shard_map/ppermute | solution.py:18
  257.5 50.8 %collective-permute-start.5 = (f32[2,3,128,6,128]{4,2,3,1,0:T(8,128)S(1)}, f32[2,3,128,6,128]{4,2,3,1,0:T(8,128)S(1)}, u32[]{:S(2)}, u32[]{:S(2)}) collective-permute-start(f32[2,3,128,6,128]{4,2,3,1,0:T(8,128)S(1)} %copy.39), channel_id=1, source_target_pairs={{6,0},{7,1},{0,2},{1,3},{2,4},{3,5},{4,6},{5,7},{14,8},{15,9},{8,1... | collective-permute-start | bytes 7077896 | tf_op jit(solution)/shard_map/ppermute | solution.py:18
  311.6 46.6 %collective-permute-start.6 = (f32[2,3,128,6,128]{4,2,3,1,0:T(8,128)}, f32[2,3,128,6,128]{4,2,3,1,0:T(8,128)}, u32[]{:S(2)}, u32[]{:S(2)}) collective-permute-start(f32[2,3,128,6,128]{4,2,3,1,0:T(8,128)} %copy.41), channel_id=1, source_target_pairs={{4,0},{5,1},{6,2},{7,3},{0,4},{1,5},{2,6},{3,7},{12,8},{13,9},{14,... | collective-permute-start | bytes 7077896 | tf_op jit(solution)/shard_map/ppermute | solution.py:18
  405.0 140.7 %all-gather.5.cloned.1.call-start = ((), (), s32[]{:S(2)}) async-start(), calls=%async_computation.1 | async-start | bytes 8912896 | tf_op jit(solution)/shard_map/all_gather | solution.py:107
  487.6 672.4 %all-reduce.6.cloned.1.call-start = ((), (), s32[]{:S(2)}) async-start(), calls=%async_computation.2 | async-start | bytes 16777216 | tf_op jit(solution)/shard_map/psum | solution.py:23
  688.5 2.2 copy-start.9
  695.8 1.5 copy-start.5
  697.3 0.7 copy-start.7
  701.8 1.0 copy-start.3
  739.5 51.2 %copy-start.4 = (f32[128,512]{0,1:T(8,128)S(1)}, f32[128,512]{0,1:T(8,128)}, u32[]{:S(2)}) copy-start(f32[128,512]{0,1:T(8,128)} %copy.49) | copy-start | bytes 786436
  739.6 51.2 %copy-start.6 = (f32[128,512]{0,1:T(8,128)S(1)}, f32[128,512]{0,1:T(8,128)}, u32[]{:S(2)}) copy-start(f32[128,512]{0,1:T(8,128)} %copy-done.5) | copy-start | bytes 786436
  739.6 51.2 %copy-start.8 = (f32[128,512]{0,1:T(8,128)S(1)}, f32[128,512]{0,1:T(8,128)}, u32[]{:S(2)}) copy-start(f32[128,512]{0,1:T(8,128)} %copy-done.7) | copy-start | bytes 786436
  909.4 3.9 copy-start.2
  927.6 5.1 copy-start
  1160.0 4.6 copy-start.1
Sparse Core Ops, SparseCore 0:
  405.1 80.5 all-gather.2
  487.9 57.6 all-gather.4
  963.5 196.4 all-reduce.5
where the time goes:
time: 1220 us; the launch traced here: 1210 us
  waiting for transfers between devices  644 us (53%)
  other arithmetic  324 us (27%)
  matrix products  117 us (10%)
  local copies, waits for them, and re-layouts  100 us (8%)
  between operations  20 us (2%)
    ppermute x7, waiting for transfers between devices, passed_along(): return lax.ppermute(block, axis, route)  313 us
    psum x1, waiting for transfers between devices, from_root(): return lax.psum(jnp.where(mine, shard, jnp.zeros_like(shard)), axis)  197 us
    another operation x29, other arithmetic, panel_factor(): jnp.linalg.cholesky(working[first_col:after_col, first_col:after_col])  159 us
    another operation x3, other arithmetic, per_device(): jax.scipy.linalg.solve_triangular(pivot_factor, jnp.eye(PIVOTS, dtype=jnp...  84.3 us
    all_gather x1, waiting for transfers between devices, per_device(): gathered = lax.all_gather(pivot_strip, 'col', axis=1, tiled=True)  80.7 us
    all_gather x1, waiting for transfers between devices, per_device(): stacked = lax.all_gather(leading, 'row', axis=0, tiled=True)  54 us
    another operation x36, local copies, waits for them, and re-layouts  42.7 us
    another operation x3, other arithmetic, panel_factor(): jax.scipy.linalg.solve_triangular(diagonal_factor, working[after_col:, fi...  41.4 us
  transfers between devices with their start and end apart: 10, of which 10 were waited for; matrix products, arithmetic and copies ran while one was open for 1% of the time, Pallas kernels for 0%

commit v1 on v0

v1 whole, which is shorter than its diff:
```python
import jax
import jax.numpy as jnp
from jax import lax
from jax.experimental import pallas as pl
from jax.experimental.pallas import tpu as pltpu
from jax.sharding import PartitionSpec as P

f32 = jnp.float32
bf16 = jnp.bfloat16
TILE = 128
RUN = 16
PIVOTS = 1024
STEPS = PIVOTS // TILE
HIGH = lax.Precision.HIGH
SUB = 8
GROUPS = TILE // SUB
ITEMS = 36
SHARE = 5
MIB = 2**20


def split2(x):
    hi = x.astype(bf16)
    return hi, (x - hi.astype(f32)).astype(bf16)


def split3(x):
    hi = x.astype(bf16).astype(f32)
    rest = x - hi
    mid = rest.astype(bf16).astype(f32)
    return hi, mid, rest - mid


def mm3(a, b, dims):
    ah, al = split2(a)
    bh, bl = split2(b)

    def dot(x, y):
        return lax.dot_general(x, y, (dims, ((), ())), preferred_element_type=f32)

    return dot(ah, bh) + (dot(ah, bl) + dot(al, bh))


def lane(x, k):
    return jnp.broadcast_to(x[:, k : k + 1], (SUB, TILE))


def sublane(x, k):
    return jnp.broadcast_to(x[k : k + 1, :], (SUB, TILE))


def factor_tile(a, e):
    row_of = lax.broadcasted_iota(jnp.int32, (SUB, TILE), 0)

    def packed(v):
        out = v[SUB - 1]
        for t in range(SUB - 2, -1, -1):
            out = jnp.where(row_of == t, v[t], out)
        return out

    inverse_rows = []
    last_u = last_e = None
    for b in range(GROUPS):
        r = [sublane(a[b], t) for t in range(SUB)]
        w = [sublane(e[b], t) for t in range(SUB)]
        if b:
            for s in range(SUB):
                for t in range(SUB):
                    factor = lane(last_u[t], SUB * b + s)
                    r[s] = r[s] - factor * last_u[t]
                    w[s] = w[s] - factor * last_e[t]
        d = [[lane(r[t], SUB * b + s) if s >= t else None for t in range(SUB)] for s in range(SUB)]
        u = [None] * SUB
        v = [None] * SUB
        for t in range(SUB):
            scale = lax.rsqrt(d[t][t])
            u[t] = r[t] * scale
            v[t] = w[t] * scale
            below = [d[s][t] * scale if s > t else None for s in range(SUB)]
            for s in range(t + 1, SUB):
                for q in range(t + 1, s + 1):
                    d[s][q] = d[s][q] - below[s] * below[q]
            for s in range(t + 1, SUB):
                r[s] = r[s] - below[s] * u[t]
                w[s] = w[s] - below[s] * v[t]
        last_u, last_e = u, v
        urows, erows = packed(u), packed(v)
        inverse_rows.append(erows)
        if b < GROUPS - 2:
            uh, um, ul = split3(urows)
            eh, em, el = split3(erows)
            left = jnp.concatenate([uh, uh, um, um, uh, ul], 0).astype(bf16)
            right = jnp.concatenate(
                [jnp.concatenate([uh, um, uh, um, ul, uh], 0), jnp.concatenate([eh, em, eh, em, el, eh], 0)], 1
            ).astype(bf16)
            change = lax.dot_general(left, right, (((0,), (0,)), ((), ())), preferred_element_type=f32)
            for i in range(b + 2, GROUPS):
                a[i] = a[i] - change[SUB * i : SUB * i + SUB, :TILE]
                e[i] = e[i] - change[SUB * i : SUB * i + SUB, TILE:]
    return jnp.concatenate(inverse_rows, 0)


def factor_kernel(block_ref, inverse_ref, work):
    width = (STEPS + 1) * TILE
    for i in range(STEPS):
        rows = slice(i * TILE, (i + 1) * TILE)
        work[rows, :PIVOTS] = block_ref[rows, :]
        ri = lax.broadcasted_iota(jnp.int32, (TILE, PIVOTS), 0) + i * TILE
        ci = lax.broadcasted_iota(jnp.int32, (TILE, PIVOTS), 1)
        work[rows, PIVOTS:] = (ri == ci).astype(f32)

    @pl.loop(0, STEPS)
    def _(k):
        kb = pl.ds(pl.multiple_of(k * TILE, TILE), TILE)
        window = pl.ds(pl.multiple_of(k * TILE, TILE), width)
        tile = work[kb, kb]
        ri = lax.broadcasted_iota(jnp.int32, (SUB, TILE), 0)
        ci = lax.broadcasted_iota(jnp.int32, (SUB, TILE), 1)
        a = [tile[SUB * i : SUB * i + SUB] for i in range(GROUPS)]
        e = [(ri + SUB * i == ci).astype(f32) for i in range(GROUPS)]
        inverse = factor_tile(a, e)
        work[kb, window] = mm3(inverse, work[kb, window], ((1,), (0,)))

        @pl.loop(k + 1, STEPS)
        def _(i):
            ib = pl.ds(pl.multiple_of(i * TILE, TILE), TILE)
            work[ib, window] -= mm3(work[kb, ib], work[kb, window], ((0,), (0,)))

    inverse_ref[...] = work[:, PIVOTS:]


def inverse_factor(block):
    vmem = pl.BlockSpec(memory_space=pltpu.VMEM)
    return pl.pallas_call(
        factor_kernel,
        out_shape=jax.ShapeDtypeStruct((PIVOTS, PIVOTS), f32),
        in_specs=[vmem],
        out_specs=vmem,
        scratch_shapes=[pltpu.VMEM((PIVOTS, 2 * PIVOTS), f32)],
        compiler_params=pltpu.CompilerParams(vmem_limit_bytes=40 * MIB),
        cost_estimate=pl.CostEstimate(flops=5 * 10**10, bytes_accessed=8 * MIB, transcendentals=0),
        name="factor",
    )(block)


def reorder_kernel(index_ref, in_ref, out_ref):
    @pl.loop(0, in_ref.shape[0])
    def _(d):
        for m in range(SHARE):
            out_ref[d, m] = in_ref[index_ref[d, m], m]


def reorder(pieces, index):
    vmem = pl.BlockSpec(memory_space=pltpu.VMEM)
    return pl.pallas_call(
        reorder_kernel,
        out_shape=jax.ShapeDtypeStruct(pieces.shape, f32),
        in_specs=[pl.BlockSpec(memory_space=pltpu.SMEM), vmem],
        out_specs=vmem,
        compiler_params=pltpu.CompilerParams(vmem_limit_bytes=16 * MIB),
        name="reorder",
    )(index, pieces)


def relay(children, child_map, rows, cols, row_index, col_index):
    pieces = children.reshape(2, 3, rows, SUB, 6, TILE).transpose(2, 0, 1, 4, 3, 5).reshape(rows, ITEMS, SUB, TILE)
    pieces = jnp.pad(pieces, ((0, 0), (0, cols * SHARE - ITEMS), (0, 0), (0, 0)))
    pieces = pieces.reshape(rows * cols, SHARE, SUB, TILE)
    held = lax.all_to_all(pieces, ("row", "col"), 0, 0, tiled=True)
    item = jnp.minimum(col_index * SHARE + jnp.arange(SHARE), ITEMS - 1)
    child, run, tile = item // 18, item % 18 // 6, item % 6
    row_start = child_map[child, run * RUN]
    col_start = child_map[child, tile // 2 * RUN]
    target = jnp.arange(rows * cols, dtype=jnp.int32)[:, None]
    index = (target // cols - row_start) % rows * cols + (target % cols - col_start) % cols
    held = reorder(held, index.astype(jnp.int32))
    back = lax.all_to_all(held, ("row", "col"), 0, 0, tiled=True)
    return back.reshape(rows, cols * SHARE, SUB, TILE)[:, :ITEMS]


def assemble_kernel(slots_ref, front_ref, items_ref, out_ref):
    out_ref[...] = front_ref[...]
    for m in range(ITEMS):
        row = pl.ds(pl.multiple_of(slots_ref[0, m] * TILE, TILE), TILE)
        col = pl.ds(pl.multiple_of(slots_ref[1, m] * TILE, TILE), TILE)
        out_ref[row, col] += items_ref[:, m].reshape(TILE, TILE)


def assemble(front, items, child_map, rows, cols, row_index, col_index):
    item = jnp.arange(ITEMS)
    child, run, tile = item // 18, item % 18 // 6, item % 6
    row_start = child_map[child, run * RUN]
    col_start = child_map[child, tile // 2 * RUN]
    row_slot = (row_start + (row_index - row_start) % rows) // rows
    col_slot = (col_start + (col_index - col_start) % cols) // cols + tile % 2
    slots = jnp.stack([row_slot, col_slot]).astype(jnp.int32)
    vmem = pl.BlockSpec(memory_space=pltpu.VMEM)
    return pl.pallas_call(
        assemble_kernel,
        out_shape=jax.ShapeDtypeStruct(front.shape, f32),
        in_specs=[pl.BlockSpec(memory_space=pltpu.SMEM), vmem, vmem],
        out_specs=vmem,
        compiler_params=pltpu.CompilerParams(vmem_limit_bytes=32 * MIB),
        name="assemble",
    )(slots, front, items)


def per_device(front, children, child_map):
    rows, cols = lax.axis_size("row"), lax.axis_size("col")
    row_index, col_index = lax.axis_index("row"), lax.axis_index("col")
    local_rows, local_cols = front.shape
    items = relay(children, child_map, rows, cols, row_index, col_index)
    assembled = assemble(front, items, child_map, rows, cols, row_index, col_index)
    row_strip = assembled[:, :TILE]
    col_strip = assembled[:TILE, :]
    half = TILE // 2
    upper = row_index < STEPS
    route = [(i, i + STEPS) for i in range(STEPS)] + [(i + STEPS, i) for i in range(STEPS)]
    second = lax.ppermute(col_strip[half:], "row", route)
    shared = jnp.where(upper, col_strip[:half], second)
    row_panel = lax.all_gather(row_strip, "col", axis=1, tiled=True)
    leading = row_panel[:TILE]
    lead_second = lax.ppermute(leading[half:], "row", route)
    lead = lax.all_gather(jnp.where(upper, leading[:half], lead_second), "row")
    block = lead.reshape(2, STEPS, half, PIVOTS).transpose(1, 0, 2, 3).reshape(PIVOTS, PIVOTS)
    col_panel = lax.all_gather(shared, "row")
    col_panel = col_panel.reshape(2, STEPS, half, local_cols).transpose(1, 0, 2, 3).reshape(PIVOTS, local_cols)
    inverse = inverse_factor(block)
    solved = jnp.dot(row_panel, inverse.T, precision=HIGH)
    row_number = jnp.arange(local_rows, dtype=jnp.int32)[:, None]
    row_number = row_number // TILE * TILE * rows + row_index * TILE + row_number % TILE
    lower_panel = jnp.where(row_number >= jnp.arange(PIVOTS)[None, :], solved, 0.0)
    update_rows = jnp.where(row_number < PIVOTS, 0.0, solved)
    update_cols = jnp.dot(inverse, col_panel, precision=HIGH)
    update_cols = jnp.where(jnp.arange(local_cols)[None, :] < TILE, 0.0, update_cols)
    front_out = assembled - jnp.dot(update_rows, update_cols, precision=HIGH)
    return front_out, lower_panel


def solution(mesh):
    return jax.shard_map(
        per_device,
        mesh=mesh,
        in_specs=(P("row", "col"), P(None, "row", "col"), P()),
        out_specs=(P("row", "col"), P("row", None)),
        check_vma=False,
    )
```

time: 1220 us -> 340 us (0.28)
  waiting for transfers between devices: 644 us -> 179 us
  other arithmetic: 324 us -> 3.96 us
  matrix products: 117 us -> 43.2 us
  local copies, waits for them, and re-layouts: 100 us -> 27.8 us
  Pallas kernels: 0 us -> 50.6 us
  starting transfers between devices: 6.9 us -> 20 us
    ppermute x7 -> x2, waiting for transfers between devices: 313 us -> 22.4 us  [the longest x1 15.4 us: per_device(): second = lax.ppermute(col_strip[half:], 'row', route)]
    another operation x36 -> x1, other arithmetic: 289 us -> 0.01 us  [assemble(): slots = jnp.stack([row_slot, col_slot]).astype(jnp.int32)]
    psum x1 -> x0, waiting for transfers between devices: 197 us -> none  [from_root(): return lax.psum(jnp.where(mine, shard, jnp.zeros_like(shard)), axis)]
    all_to_all x0 -> x2, waiting for transfers between devices: none -> 64.7 us  [the longest x1 32.6 us: relay(): held = lax.all_to_all(pieces, ('row', 'col'), 0, 0, tiled=True)]
    pallas_call x0 -> x3, Pallas kernels: none -> 50.6 us  [the longest x1 46.1 us: inverse_factor(): pl.pallas_call(factor_kernel, out_shape=jax.ShapeDtypeStruct((PIVOTS, PIV...]
    another operation x49 -> x0, local copies, waits for them, and re-layouts: 44.1 us -> none
    all_gather x2 -> x3, waiting for transfers between devices: 135 us -> 91.6 us  [the longest x1 71.4 us: per_device(): row_panel = lax.all_gather(row_strip, 'col', axis=1, tiled=True)]
    another operation x34 -> x0, matrix products: 38.3 us -> none  [the longest x15 23.1 us: per_device(): jax.scipy.linalg.solve_triangular(pivot_factor, jnp.eye(PIVOTS, dtype=jnp...]
  transfers between devices with their start and end apart: 10 -> 7, of which waited for: 10 -> 6; matrix products, arithmetic and copies ran while one was open for 1% -> 6% of each run, Pallas kernels for 0% -> 14%
where the time goes in v1:
time: 340 us; the launch traced here: 338 us
  waiting for transfers between devices  179 us (53%)
  Pallas kernels  50.6 us (15%)
  matrix products  43.2 us (13%)
  local copies, waits for them, and re-layouts  27.8 us (8%)
  starting transfers between devices  20 us (6%)
  between operations  14 us (4%)
  other arithmetic  3.96 us (1%)
    all_gather x1, waiting for transfers between devices, per_device(): row_panel = lax.all_gather(row_strip, 'col', axis=1, tiled=True)  71.4 us
    pallas_call x1, Pallas kernels, inverse_factor(): pl.pallas_call(factor_kernel, out_shape=jax.ShapeDtypeStruct((PIVOTS, PIV...  46.1 us
    all_to_all x1, waiting for transfers between devices, relay(): held = lax.all_to_all(pieces, ('row', 'col'), 0, 0, tiled=True)  32.6 us
    all_to_all x1, waiting for transfers between devices, relay(): back = lax.all_to_all(held, ('row', 'col'), 0, 0, tiled=True)  32 us
    all_gather x1, waiting for transfers between devices, per_device(): lead = lax.all_gather(jnp.where(upper, leading[:half], lead_second), 'row')  20.2 us
    dot_general x1, matrix products, per_device(): front_out = assembled - jnp.dot(update_rows, update_cols, precision=HIGH)  18.3 us
    dot_general x1, matrix products, per_device(): update_cols = jnp.dot(inverse, col_panel, precision=HIGH)  15.8 us
    ppermute x1, waiting for transfers between devices, per_device(): second = lax.ppermute(col_strip[half:], 'row', route)  15.4 us
  transfers between devices with their start and end apart: 7, of which 6 were waited for; matrix products, arithmetic and copies ran while one was open for 6% of the time, Pallas kernels for 14%

profile of v1, /device:TPU:7, one launch (start us, length us, event | category | flops | bytes accessed | tf_op | source)
XLA Modules:
  0.0 338.3 jit_solution(6737208146900873141)
XLA Ops:
  7.2 1.9 copy.7
  9.1 1.8 pad.4
  10.9 10.8 %all-to-all-start = ((f32[128,5,8,128]{3,2,1,0:T(8,128)}), f32[128,5,8,128]{3,2,1,0:T(8,128)S(1)}, u32[]{:S(2)}, u32[]{:S(2)}) async-start(f32[128,5,8,128]{3,2,1,0:T(8,128)} %bitcast.45), calls=%async_computation | async-start | bytes 5242880 | tf_op jit(solution)/shard_map/all_to_all | solution.py:169
  23.3 32.6 %all-to-all-done.in_ref = f32[128,5,8,128]{3,2,1,0:T(8,128)S(1)} async-done(((f32[128,5,8,128]{3,2,1,0:T(8,128)}), f32[128,5,8,128]{3,2,1,0:T(8,128)S(1)}, u32[]{:S(2)}, u32[]{:S(2)}) %all-to-all-start) | async-done | bytes 2621472 | tf_op jit(solution)/shard_map/all_to_all | solution.py:169
  55.9 2.9 reorder.1
  58.8 1.5 copy-done.3
  60.3 6.4 %all-to-all-start.1 = ((f32[128,5,8,128]{3,2,1,0:T(8,128)}), f32[128,5,8,128]{3,2,1,0:T(8,128)S(1)}, u32[]{:S(2)}, u32[]{:S(2)}) async-start(f32[128,5,8,128]{3,2,1,0:T(8,128)} %copy-done.3), calls=%async_computation.1 | async-start | bytes 5242880 | tf_op jit(solution)/shard_map/all_to_all | solution.py:177
  69.0 32.0 %all-to-all-done.1 = f32[128,5,8,128]{3,2,1,0:T(8,128)S(1)} async-done(((f32[128,5,8,128]{3,2,1,0:T(8,128)}), f32[128,5,8,128]{3,2,1,0:T(8,128)S(1)}, u32[]{:S(2)}, u32[]{:S(2)}) %all-to-all-start.1) | async-done | bytes 2621472 | tf_op jit(solution)/shard_map/all_to_all | solution.py:177
  101.2 3.4 copy-done.4
  104.6 1.6 assemble.1
  106.2 3.4 %copy-done.2 = f32[1024,2048]{1,0:T(8,128)} copy-done((f32[1024,2048]{1,0:T(8,128)}, f32[1024,2048]{1,0:T(8,128)S(1)}, u32[]{:S(2)}) %copy-start.2) | copy-done | bytes 8388632
  110.5 71.4 %all-gather.6.cloned.1.call-done = f32[1024,1024]{1,0:T(8,128)} async-done(((f32[1024,128]{1,0:T(8,128)}), f32[1024,1024]{1,0:T(8,128)}) %all-gather.6.cloned.1.call-update) | async-done | bytes 4194320 | tf_op jit(solution)/shard_map/all_gather | solution.py:221
  184.1 7.1 %collective-permute-done = f32[64,1024]{1,0:T(8,128)S(1)} collective-permute-done((f32[64,1024]{1,0:T(8,128)S(1)}, f32[64,1024]{1,0:T(8,128)S(1)}, u32[]{:S(2)}, u32[]{:S(2)}) %collective-permute-start) | collective-permute-done | bytes 262176 | tf_op jit(solution)/shard_map/ppermute | solution.py:223
  191.2 1.7 slice_select_fusion.1
  195.5 15.4 %collective-permute-done.1 = f32[64,2048]{1,0:T(8,128)S(1)} collective-permute-done((f32[64,2048]{1,0:T(8,128)S(1)}, f32[64,2048]{1,0:T(8,128)S(1)}, u32[]{:S(2)}, u32[]{:S(2)}) %collective-permute-start.1) | collective-permute-done | bytes 524320 | tf_op jit(solution)/shard_map/ppermute | solution.py:219
  210.9 2.0 slice_select_fusion
  212.9 20.2 %all-gather.8.cloned.1.call-done = f32[1024,1024]{1,0:T(8,128)} async-done(((f32[64,1024]{1,0:T(8,128)}), f32[1024,1024]{1,0:T(8,128)}) %all-gather.8.cloned.1.call-update) | async-done | bytes 4194320 | tf_op jit(solution)/shard_map/all_gather | solution.py:224
  233.1 2.8 copy.8
  235.9 46.1 %factor.1 = f32[1024,1024]{1,0:T(8,128)S(1)} custom-call(f32[1024,1024]{1,0:T(8,128)S(1)} %bitcast.44), custom_call_target="tpu_custom_call" | custom-call | flops 49999998976 | bytes 8388608 | tf_op jit(solution)/shard_map/factor/pallas_call | solution.py:134
  282.0 1.9 copy-done.5
  284.0 9.1 %fusion.4 = (f32[1024,1024]{1,0:T(8,128)}, f32[1024,1024]{1,0:T(8,128)}) fusion(s32[1024]{0:T(1024)S(1)} %fusion.25, f32[1024,1024]{1,0:T(8,128)S(1)} %copy-done.7, f32[1024,1024]{1,0:T(8,128)S(1)} %factor.1), kind=kOutput, calls=%fused_computation.9 | convolution fusion | flops 6444548096 | bytes 16781312 | tf_op jit(solution)/shard_map/dot_general | solution.py:229
  293.0 4.1 %copy.9 = f32[2,8,64,2048]{3,2,0,1:T(8,128)S(1)} copy(f32[2,8,64,2048]{3,2,1,0:T(8,128)} %bitcast.48) | data formatting | bytes 16777216 | tf_op jit(solution)/shard_map/reshape | solution.py:227
  297.6 15.8 %fusion.54 = f32[1024,2048]{1,0:T(8,128)} fusion(f32[1024,1024]{1,0:T(8,128)S(1)} %copy-done.6, f32[1024,2048]{1,0:T(8,128)S(1)} %bitcast.49), kind=kOutput, calls=%fused_computation.125 | convolution fusion | flops 12884901888 | bytes 20971520 | tf_op jit(solution)/shard_map/dot_general | solution.py:234
  313.4 18.3 %fusion.6 = f32[1024,2048]{1,0:T(8,128)} fusion(f32[1024,2048]{1,0:T(8,128)S(1)} %bitcast.43, f32[1024,2048]{1,0:T(8,128)} %fusion.54, pred[2048]{0:T(1024)(128)(4,1)S(1)} %iota_compare_fusion.1, f32[1024,1024]{1,0:T(8,128)} %get-tuple-element.3, pred[1024]{0:T(1024)(128)(4,1)S(1)} %broadcast_compare_fusion), kind=kOutput, calls=%fused_computation.11 | convolution fusion | flops 12890144768 | bytes 29363200 | tf_op jit(solution)/shard_map/dot_general | solution.py:236
  (44 shorter events, 10.2 us)
Async XLA Ops:
  7.2 14.6 %copy-start = (s32[2,48]{1,0:T(2,128)S(1)}, s32[2,48]{1,0:T(2,128)}, u32[]{:S(2)}) copy-start(s32[2,48]{1,0:T(2,128)} %param.5) | copy-start | bytes 1156
  10.9 45.0 %all-to-all-start = ((f32[128,5,8,128]{3,2,1,0:T(8,128)}), f32[128,5,8,128]{3,2,1,0:T(8,128)S(1)}, u32[]{:S(2)}, u32[]{:S(2)}) async-start(f32[128,5,8,128]{3,2,1,0:T(8,128)} %bitcast.45), calls=%async_computation | async-start | bytes 5242880 | tf_op jit(solution)/shard_map/all_to_all | solution.py:169
  58.8 1.5 copy-start.3
  60.3 40.7 %all-to-all-start.1 = ((f32[128,5,8,128]{3,2,1,0:T(8,128)}), f32[128,5,8,128]{3,2,1,0:T(8,128)S(1)}, u32[]{:S(2)}, u32[]{:S(2)}) async-start(f32[128,5,8,128]{3,2,1,0:T(8,128)} %copy-done.3), calls=%async_computation.1 | async-start | bytes 5242880 | tf_op jit(solution)/shard_map/all_to_all | solution.py:177
  66.7 115.2 %all-gather.6.cloned.1.call-start = ((), (), s32[]{:S(2)}) async-start(), calls=%async_computation.2 | async-start | bytes 4718592 | tf_op jit(solution)/shard_map/all_gather | solution.py:221
  101.2 3.4 %copy-start.4 = (f32[1024,2048]{1,0:T(8,128)S(1)}, f32[1024,2048]{1,0:T(8,128)}, u32[]{:S(2)}) copy-start(f32[1024,2048]{1,0:T(8,128)} %front_ref.1) | copy-start | bytes 25165828
  106.2 3.4 %copy-start.2 = (f32[1024,2048]{1,0:T(8,128)}, f32[1024,2048]{1,0:T(8,128)S(1)}, u32[]{:S(2)}) copy-start(f32[1024,2048]{1,0:T(8,128)S(1)} %assemble.1) | copy-start | bytes 25165828
  110.5 122.6 %all-gather.8.cloned.1.call-start = ((), (), s32[]{:S(2)}) async-start(), calls=%async_computation.3 | async-start | bytes 4456448 | tf_op jit(solution)/shard_map/all_gather | solution.py:224
  182.9 8.3 %collective-permute-start = (f32[64,1024]{1,0:T(8,128)S(1)}, f32[64,1024]{1,0:T(8,128)S(1)}, u32[]{:S(2)}, u32[]{:S(2)}) collective-permute-start(f32[64,1024]{1,0:T(8,128)S(1)} %slice.41), channel_id=1, source_target_pairs={{0,64},{8,72},{16,80},{24,88},{32,96},{40,104},{48,112},{56,120},{... | collective-permute-start | bytes 786440 | tf_op jit(solution)/shard_map/ppermute | solution.py:223
  192.9 100.1 %all-gather.10.cloned.1.call-start = ((), (), s32[]{:S(2)}) async-start(), calls=%async_computation.4 | async-start | bytes 8912896 | tf_op jit(solution)/shard_map/all_gather | solution.py:226
  194.1 16.8 %collective-permute-start.1 = (f32[64,2048]{1,0:T(8,128)S(1)}, f32[64,2048]{1,0:T(8,128)S(1)}, u32[]{:S(2)}, u32[]{:S(2)}) collective-permute-start(f32[64,2048]{1,0:T(8,128)S(1)} %slice.43), channel_id=1, source_target_pairs={{0,64},{8,72},{16,80},{24,88},{32,96},{40,104},{48,112},{56,120},{... | collective-permute-start | bytes 1572872 | tf_op jit(solution)/shard_map/ppermute | solution.py:219
  235.9 48.1 %copy-start.7 = (f32[1024,1024]{1,0:T(8,128)S(1)}, f32[1024,1024]{1,0:T(8,128)}, u32[]{:S(2)}) copy-start(f32[1024,1024]{1,0:T(8,128)} %all-gather.6.cloned.1.call-done) | copy-start | bytes 12582916
  282.0 2.0 copy-start.5
  293.0 4.6 %copy-start.6 = (f32[1024,1024]{1,0:T(8,128)S(1)}, f32[1024,1024]{1,0:T(8,128)}, u32[]{:S(2)}) copy-start(f32[1024,1024]{1,0:T(8,128)} %copy-done.5) | copy-start | bytes 12582916
  293.0 20.4 %slice-start = ((s8[8388608]{0:T(1024)(128)(4,1)}), s8[4194304]{0:T(1024)(128)(4,1)S(1)}, s32[]{:S(2)}) async-start(s8[8388608]{0:T(1024)(128)(4,1)} %bitcast.42), calls=%async_computation.5 | async-start | bytes 8388608
  297.6 15.8 %slice-start.1 = ((s8[8388608]{0:T(1024)(128)(4,1)}), s8[4194304]{0:T(1024)(128)(4,1)S(1)}, s32[]{:S(2)}) async-start(s8[8388608]{0:T(1024)(128)(4,1)} %bitcast.42), calls=%async_computation.6 | async-start | bytes 8388608
  313.4 18.4 %copy-start.1 = (s32[2,48]{1,0:T(2,128)S(1)}, s32[2,48]{1,0:T(2,128)}, u32[]{:S(2)}) copy-start(s32[2,48]{1,0:T(2,128)} %param.5) | copy-start | bytes 1156
Sparse Core Ops, SparseCore 0:
  110.6 71.2 all-gather.5
  193.0 40.0 all-gather.7
  234.8 51.0 all-gather.9

commit v2 on v1

--- a/solution.py
+++ b/solution.py
@@ -11,7 +11,6 @@
 RUN = 16
 PIVOTS = 1024
 STEPS = PIVOTS // TILE
-HIGH = lax.Precision.HIGH
 SUB = 8
 GROUPS = TILE // SUB
 ITEMS = 36
@@ -100,17 +99,26 @@
     return jnp.concatenate(inverse_rows, 0)
 
 
-def factor_kernel(block_ref, inverse_ref, work):
-    width = (STEPS + 1) * TILE
+def load_block(pivots, work):
+    for x in range(2):
+        for y in range(4):
+            for z in range(4):
+                for core in range(2):
+                    i = x * 4 + y % 2 * 2 + core
+                    j = y // 2 * 4 + z
+                    work[i * TILE : (i + 1) * TILE, j * TILE : (j + 1) * TILE] = pivots[core, x, y, z]
     for i in range(STEPS):
-        rows = slice(i * TILE, (i + 1) * TILE)
-        work[rows, :PIVOTS] = block_ref[rows, :]
         ri = lax.broadcasted_iota(jnp.int32, (TILE, PIVOTS), 0) + i * TILE
         ci = lax.broadcasted_iota(jnp.int32, (TILE, PIVOTS), 1)
-        work[rows, PIVOTS:] = (ri == ci).astype(f32)
+        work[i * TILE : (i + 1) * TILE, PIVOTS:] = (ri == ci).astype(f32)
+
+
+def factor_steps(work, between):
+    width = (STEPS + 1) * TILE
 
     @pl.loop(0, STEPS)
     def _(k):
+        between(k)
         kb = pl.ds(pl.multiple_of(k * TILE, TILE), TILE)
         window = pl.ds(pl.multiple_of(k * TILE, TILE), width)
         tile = work[kb, kb]
@@ -126,21 +134,363 @@
             ib = pl.ds(pl.multiple_of(i * TILE, TILE), TILE)
             work[ib, window] -= mm3(work[kb, ib], work[kb, window], ((0,), (0,)))
 
-    inverse_ref[...] = work[:, PIVOTS:]
-
-
-def inverse_factor(block):
+
+class Exchange:
+    def __init__(self, send_sems, recv_sems):
+        self.send_sems, self.recv_sems, self.used = send_sems, recv_sems, 0
+        self.sent = []
+
+    def copy(self, ref, out_at, in_at, device, sends=None, receives=None, source=None):
+        n = self.used
+        self.used += 1
+
+        def made(at, src):
+            return pltpu.make_async_remote_copy(
+                src_ref=src,
+                dst_ref=ref.at[at],
+                send_sem=self.send_sems.at[n],
+                recv_sem=self.recv_sems.at[n],
+                device_id=device,
+                device_id_type=pl.DeviceIdType.MESH,
+            )
+
+        def start():
+            made(out_at, ref.at[out_at] if source is None else source).start()
+
+        def wait_recv():
+            made(in_at, ref.at[in_at]).wait_recv()
+
+        def wait_send():
+            made(out_at, ref.at[out_at] if source is None else source).wait_send()
+
+        self.sent.append((sends, wait_send))
+        return (sends, start), (receives, wait_recv)
+
+    def drain(self):
+        for guard, wait in self.sent:
+            guarded(guard, wait)
+
+
+def guarded(guard, action):
+    if guard is None:
+        action()
+    else:
+        pl.when(guard)(action)
+
+
+def begin(copies):
+    for (guard, start), _ in copies:
+        guarded(guard, start)
+    return copies
+
+
+def finish(copies):
+    for _, (guard, wait) in copies:
+        guarded(guard, wait)
+
+
+def gather_kernel(strip_ref, cols_ref, xh_ref, xl_ref, wrow_ref, wcol_ref, pivots, work, send_sems, recv_sems):
+    r, c = lax.axis_index("row"), lax.axis_index("col")
+    x, yl, core = r // 4, r // 2 % 2, r % 2
+    yh, z = c // 4, c % 4
+    y = yh * 2 + yl
+    at = {"x": x, "y": y, "z": z}
+    near = x < 2
+    xs = x % 2
+
+    def device(x=x, y=y, z=z, core=core):
+        return (x * 4 + y % 2 * 2 + core, y // 2 * 4 + z)
+
+    def moved(dim, step):
+        return (at[dim] + step) % 4
+
+    barrier = pltpu.get_barrier_semaphore()
+    for dim in "xyz":
+        for step in range(1, 4):
+            pl.semaphore_signal(
+                barrier, inc=1, device_id=device(**{dim: moved(dim, step)}), device_id_type=pl.DeviceIdType.MESH
+            )
+    pl.semaphore_signal(barrier, inc=1, device_id=device(core=1 - core), device_id_type=pl.DeviceIdType.MESH)
+
+    @pl.when(near)
+    def _():
+        pivots[core, xs, y, z] = strip_ref[:TILE, :]
+        wcol_ref[r % 8] = cols_ref[...]
+
+    wrow_ref[:, pl.ds(pl.multiple_of(c * TILE, TILE), TILE)] = strip_ref[...]
+    pl.semaphore_wait(barrier, 10)
+    ex = Exchange(send_sems, recv_sems)
+
+    def pivot_phase(rows, order, number):
+        dim, done = order[number], order[:number]
+        waits = []
+        for step in range(1, 4):
+
+            def block(**over):
+                place = {"x": xs, "y": y, "z": z, **over}
+                full = {"x": pl.ds(0, 2), "y": pl.ds(0, 4), "z": pl.ds(0, 4)}
+                index = [full[d] if d in done else place[d] for d in "xyz"]
+                return (core, *index, pl.ds(rows[0], rows[1] - rows[0]))
+
+            source = moved(dim, -step)
+            if "x" in done:
+                sends = receives = None
+            elif dim == "x":
+                sends, receives = near, source < 2
+            else:
+                sends = receives = near
+            waits.append(
+                ex.copy(
+                    pivots,
+                    block(),
+                    block(**{dim: source % 2 if dim == "x" else source}),
+                    device(**{dim: moved(dim, step)}),
+                    sends,
+                    receives,
+                )
+            )
+        return begin(waits)
+
+    def pivot_swap(rows):
+        def block(k):
+            full = (pl.ds(0, 2), pl.ds(0, 4), pl.ds(0, 4))
+            return (k, *full, pl.ds(rows[0], rows[1] - rows[0]))
+
+        return begin([ex.copy(pivots, block(core), block(1 - core), device(core=1 - core))])
+
+    parts = (((0, 48), "xyz"), ((48, 96), "zxy"), ((96, 128), "yzx"))
+    pending = [pivot_phase(rows, order, 0) for rows, order in parts]
+    for number in (1, 2):
+        for p, (rows, order) in enumerate(parts):
+            finish(pending[p])
+            pending[p] = pivot_phase(rows, order, number)
+    for p, (rows, order) in enumerate(parts):
+        finish(pending[p])
+        pending[p] = pivot_swap(rows)
+
+    low, high = (pl.ds(0, 512), pl.ds(512, 512))
+    left, right = (pl.ds(0, 1024), pl.ds(1024, 1024))
+
+    def tiles(first, count):
+        return pl.ds(pl.multiple_of(first * TILE, TILE), count * TILE)
+
+    def owner(x, yl):
+        return x * 4 + yl * 2 + core
+
+    first_row = [ex.copy(wrow_ref, (low, tiles(c, 1)), (low, tiles((c + 4) % 8, 1)), device(y=(y + 2) % 4))]
+    second_row = [
+        ex.copy(
+            wrow_ref,
+            (high, tiles(c, 1)),
+            (high, tiles(yh * 4 + moved("z", -step), 1)),
+            device(z=moved("z", step)),
+        )
+        for step in range(1, 4)
+    ]
+    first_col = [
+        ex.copy(
+            wcol_ref,
+            (owner(xs, yl), pl.ds(0, TILE), left),
+            (owner(moved("x", -step) % 2, yl), pl.ds(0, TILE), left),
+            device(x=moved("x", step)),
+            near,
+            moved("x", -step) < 2,
+        )
+        for step in range(1, 4)
+    ]
+    y_pair = yh * 2 + 1 - yl
+    second_col = [
+        ex.copy(
+            wcol_ref,
+            (owner(xs, yl), pl.ds(0, TILE), right),
+            (owner(xs, 1 - yl), pl.ds(0, TILE), right),
+            device(y=y_pair),
+            near,
+            near,
+        )
+    ]
+    for copies in (first_row, second_row, first_col, second_col):
+        begin(copies)
+    for p in range(3):
+        finish(pending[p])
+    load_block(pivots, work)
+    last_row = [
+        ex.copy(
+            wrow_ref,
+            (low, tiles(h * 4 + z, 1)),
+            (low, tiles(h * 4 + moved("z", -step), 1)),
+            device(z=moved("z", step)),
+        )
+        for step in range(1, 4)
+        for h in range(2)
+    ]
+    side_row = [ex.copy(wrow_ref, (high, tiles(yh * 4, 4)), (high, tiles((1 - yh) * 4, 4)), device(y=(y + 2) % 4))]
+    far_col = [
+        ex.copy(
+            wcol_ref,
+            (owner(xs, h), pl.ds(0, TILE), right),
+            (owner(moved("x", -step) % 2, h), pl.ds(0, TILE), right),
+            device(x=moved("x", step)),
+            near,
+            moved("x", -step) < 2,
+        )
+        for step in range(1, 4)
+        for h in range(2)
+    ]
+    side_col = [
+        ex.copy(wcol_ref, (owner(h, yl), pl.ds(0, TILE), left), (owner(h, 1 - yl), pl.ds(0, TILE), left), device(y=y_pair))
+        for h in range(2)
+    ]
+    swaps = [
+        [
+            ex.copy(
+                wcol_ref,
+                (4 * a + 2 * b + core, pl.ds(0, TILE), half),
+                (4 * a + 2 * b + 1 - core, pl.ds(0, TILE), half),
+                device(core=1 - core),
+            )
+            for a in range(2)
+            for b in range(2)
+        ]
+        for half in (left, right)
+    ]
+
+    def middle():
+        finish(first_row)
+        begin(last_row)
+        finish(second_row)
+        begin(side_row)
+        finish(second_col)
+        begin(far_col)
+        finish(first_col)
+        begin(side_col)
+
+    def swap_cols():
+        for copies, swap in ((side_col, swaps[0]), (far_col, swaps[1])):
+            finish(copies)
+            begin(swap)
+
+    def between(k):
+        pl.when(k == 3)(middle)
+        pl.when(k == 6)(swap_cols)
+
+    if OVERLAP:
+        factor_steps(work, between)
+    else:
+        middle()
+        swap_cols()
+        factor_steps(work, lambda k: None)
+    finish(last_row)
+    finish(side_row)
+    finish(swaps[0])
+    finish(swaps[1])
+    ex.drain()
+    for i in range(STEPS):
+        rows = slice(i * TILE, (i + 1) * TILE)
+        xh_ref[rows], xl_ref[rows] = split2(work[rows, PIVOTS:])
+
+
+OVERLAP = True
+COPIES = 80
+
+
+def gather_and_factor(row_strip, col_strip):
     vmem = pl.BlockSpec(memory_space=pltpu.VMEM)
+    local_rows, local_cols = row_strip.shape[0], col_strip.shape[1]
+    half = jax.ShapeDtypeStruct((PIVOTS, PIVOTS), bf16)
     return pl.pallas_call(
-        factor_kernel,
-        out_shape=jax.ShapeDtypeStruct((PIVOTS, PIVOTS), f32),
-        in_specs=[vmem],
-        out_specs=vmem,
-        scratch_shapes=[pltpu.VMEM((PIVOTS, 2 * PIVOTS), f32)],
+        gather_kernel,
+        out_shape=(
+            half,
+            half,
+            jax.ShapeDtypeStruct((local_rows, PIVOTS), f32),
+            jax.ShapeDtypeStruct((STEPS, TILE, local_cols), f32),
+        ),
+        in_specs=[vmem] * 2,
+        out_specs=(vmem,) * 4,
+        scratch_shapes=[
+            pltpu.VMEM((2, 2, 4, 4, TILE, TILE), f32),
+            pltpu.VMEM((PIVOTS, 2 * PIVOTS), f32),
+            pltpu.SemaphoreType.DMA((COPIES,)),
+            pltpu.SemaphoreType.DMA((COPIES,)),
+        ],
+        compiler_params=pltpu.CompilerParams(
+            vmem_limit_bytes=48 * MIB, collective_id=0, has_side_effects=True
+        ),
+        cost_estimate=pl.CostEstimate(flops=5 * 10**10, bytes_accessed=8 * MIB, transcendentals=0),
+        name="gather_factor",
+    )(row_strip, col_strip)
+
+
+def dot3(ah, al, bh, bl, dims):
+    def dot(p, q):
+        return lax.dot_general(p, q, (dims, ((), ())), preferred_element_type=f32)
+
+    return dot(ah, bh) + (dot(ah, bl) + dot(al, bh))
+
+
+QUARTER = 256
+
+
+def solve_rows_kernel(place_ref, w_ref, xh_ref, xl_ref, lower_ref, uh_ref, ul_ref):
+    step = pl.program_id(0)
+    wh, wl = split2(w_ref[...])
+    count = w_ref.shape[0]
+    for n in range(PIVOTS // QUARTER):
+        block = slice(n * QUARTER, (n + 1) * QUARTER)
+        depth = slice(0, (n + 1) * QUARTER)
+        b = dot3(wh[:, depth], wl[:, depth], xh_ref[block, depth], xl_ref[block, depth], ((1,), (1,)))
+        row = lax.broadcasted_iota(jnp.int32, b.shape, 0)
+        row = row % TILE + (row // TILE + step * (count // TILE)) * (TILE * place_ref[0]) + place_ref[1] * TILE
+        col = lax.broadcasted_iota(jnp.int32, b.shape, 1) + n * QUARTER
+        lower_ref[:, block] = jnp.where(row >= col, b, 0.0)
+        uh_ref[:, block], ul_ref[:, block] = split2(jnp.where(row < PIVOTS, 0.0, b))
+
+
+def solve_rows(place, panel, xh, xl):
+    rows = panel.shape[0]
+    whole = pl.BlockSpec((PIVOTS, PIVOTS), lambda i: (0, 0))
+    block = pl.BlockSpec((QUARTER, PIVOTS), lambda i: (i, 0))
+    half = jax.ShapeDtypeStruct((rows, PIVOTS), bf16)
+    return pl.pallas_call(
+        solve_rows_kernel,
+        grid=(rows // QUARTER,),
+        out_shape=(jax.ShapeDtypeStruct((rows, PIVOTS), f32), half, half),
+        in_specs=[pl.BlockSpec(memory_space=pltpu.SMEM), block, whole, whole],
+        out_specs=(block,) * 3,
         compiler_params=pltpu.CompilerParams(vmem_limit_bytes=40 * MIB),
-        cost_estimate=pl.CostEstimate(flops=5 * 10**10, bytes_accessed=8 * MIB, transcendentals=0),
-        name="factor",
-    )(block)
+        name="solve_rows",
+    )(place, panel, xh, xl)
+
+
+def update_kernel(front_ref, w_ref, xh_ref, xl_ref, uh_ref, ul_ref, out_ref, bh, bl):
+    wh, wl = split2(w_ref[...].reshape(PIVOTS, QUARTER))
+    for n in range(PIVOTS // QUARTER):
+        block = slice(n * QUARTER, (n + 1) * QUARTER)
+        depth = slice(0, (n + 1) * QUARTER)
+        b = dot3(xh_ref[block, depth], xl_ref[block, depth], wh[depth], wl[depth], ((1,), (0,)))
+        col = lax.broadcasted_iota(jnp.int32, b.shape, 1) + pl.program_id(0) * QUARTER
+        bh[block], bl[block] = split2(jnp.where(col < TILE, 0.0, b))
+    for n in range(front_ref.shape[0] // QUARTER):
+        block = slice(n * QUARTER, (n + 1) * QUARTER)
+        out_ref[block] = front_ref[block] - dot3(uh_ref[block], ul_ref[block], bh[...], bl[...], ((1,), (0,)))
+
+
+def update(front, panel, xh, xl, uh, ul):
+    rows, cols = front.shape
+    whole = pl.BlockSpec((PIVOTS, PIVOTS), lambda j: (0, 0))
+    rows_whole = pl.BlockSpec((rows, PIVOTS), lambda j: (0, 0))
+    block = pl.BlockSpec((rows, QUARTER), lambda j: (0, j))
+    return pl.pallas_call(
+        update_kernel,
+        grid=(cols // QUARTER,),
+        out_shape=jax.ShapeDtypeStruct(front.shape, f32),
+        in_specs=[block, pl.BlockSpec((STEPS, TILE, QUARTER), lambda j: (0, 0, j)), whole, whole, rows_whole, rows_whole],
+        out_specs=block,
+        scratch_shapes=[pltpu.VMEM((PIVOTS, QUARTER), bf16)] * 2,
+        compiler_params=pltpu.CompilerParams(vmem_limit_bytes=40 * MIB),
+        name="update",
+    )(front, panel, xh, xl, uh, ul)
 
 
 def reorder_kernel(index_ref, in_ref, out_ref):
@@ -211,29 +561,10 @@
     local_rows, local_cols = front.shape
     items = relay(children, child_map, rows, cols, row_index, col_index)
     assembled = assemble(front, items, child_map, rows, cols, row_index, col_index)
-    row_strip = assembled[:, :TILE]
-    col_strip = assembled[:TILE, :]
-    half = TILE // 2
-    upper = row_index < STEPS
-    route = [(i, i + STEPS) for i in range(STEPS)] + [(i + STEPS, i) for i in range(STEPS)]
-    second = lax.ppermute(col_strip[half:], "row", route)
-    shared = jnp.where(upper, col_strip[:half], second)
-    row_panel = lax.all_gather(row_strip, "col", axis=1, tiled=True)
-    leading = row_panel[:TILE]
-    lead_second = lax.ppermute(leading[half:], "row", route)
-    lead = lax.all_gather(jnp.where(upper, leading[:half], lead_second), "row")
-    block = lead.reshape(2, STEPS, half, PIVOTS).transpose(1, 0, 2, 3).reshape(PIVOTS, PIVOTS)
-    col_panel = lax.all_gather(shared, "row")
-    col_panel = col_panel.reshape(2, STEPS, half, local_cols).transpose(1, 0, 2, 3).reshape(PIVOTS, local_cols)
-    inverse = inverse_factor(block)
-    solved = jnp.dot(row_panel, inverse.T, precision=HIGH)
-    row_number = jnp.arange(local_rows, dtype=jnp.int32)[:, None]
-    row_number = row_number // TILE * TILE * rows + row_index * TILE + row_number % TILE
-    lower_panel = jnp.where(row_number >= jnp.arange(PIVOTS)[None, :], solved, 0.0)
-    update_rows = jnp.where(row_number < PIVOTS, 0.0, solved)
-    update_cols = jnp.dot(inverse, col_panel, precision=HIGH)
-    update_cols = jnp.where(jnp.arange(local_cols)[None, :] < TILE, 0.0, update_cols)
-    front_out = assembled - jnp.dot(update_rows, update_cols, precision=HIGH)
+    xh, xl, row_panel, col_panel = gather_and_factor(assembled[:, :TILE], assembled[:TILE, :])
+    place = jnp.stack([jnp.int32(rows), row_index])
+    lower_panel, uh, ul = solve_rows(place, row_panel, xh, xl)
+    front_out = update(assembled, col_panel, xh, xl, uh, ul)
     return front_out, lower_panel
 
 

time: 340 us -> 255 us (0.75)
  waiting for transfers between devices: 179 us -> 64.6 us
  Pallas kernels: 50.6 us -> 154 us
  matrix products: 43.2 us -> 0 us
  between operations: 14 us -> 0.8 us
  local copies, waits for them, and re-layouts: 27.8 us -> 17.7 us
  other arithmetic: 3.96 us -> 0.34 us
    pallas_call x1 -> x3, Pallas kernels: 46.1 us -> 149 us  [the longest x1 117 us: gather_and_factor(): pl.pallas_call(gather_kernel, out_shape=(half, half, jax.ShapeDtypeStruct...]
    all_gather x3 -> x0, waiting for transfers between devices: 91.6 us -> none  [the longest x1 71.4 us: per_device(): row_panel = lax.all_gather(row_strip, 'col', axis=1, tiled=True)]
    dot_general x3 -> x0, matrix products: 43.2 us -> none  [the longest x1 18.3 us: per_device(): front_out = assembled - jnp.dot(update_rows, update_cols, precision=HIGH)]
    ppermute x2 -> x0, waiting for transfers between devices: 22.4 us -> none  [the longest x1 15.4 us: per_device(): second = lax.ppermute(col_strip[half:], 'row', route)]
    reshape x2 -> x0, local copies, waits for them, and re-layouts: 6.89 us -> none  [the longest x1 4.13 us: per_device(): col_panel.reshape(2, STEPS, half, local_cols).transpose(1, 0, 2, 3)]
    select_n x2 -> x0, other arithmetic: 3.67 us -> none  [the longest x1 1.97 us: per_device(): shared = jnp.where(upper, col_strip[:half], second)]
    unnamed x20 -> x12, local copies, waits for them, and re-layouts: 10.7 us -> 10.2 us
  transfers between devices with their start and end apart: 7 -> 2, of which waited for: 6 -> 2; matrix products, arithmetic and copies ran while one was open for 6% -> 1% of each run, Pallas kernels for 14% -> 0%
where the time goes in v2:
time: 255 us; the launch traced here: 254 us
  Pallas kernels  154 us (60%)
  waiting for transfers between devices  64.6 us (25%)
  local copies, waits for them, and re-layouts  17.7 us (7%)
  starting transfers between devices  17.2 us (7%)
    pallas_call x1, Pallas kernels, gather_and_factor(): pl.pallas_call(gather_kernel, out_shape=(half, half, jax.ShapeDtypeStruct...  117 us
    all_to_all x1, waiting for transfers between devices, relay(): held = lax.all_to_all(pieces, ('row', 'col'), 0, 0, tiled=True)  32.6 us
    all_to_all x1, waiting for transfers between devices, relay(): back = lax.all_to_all(held, ('row', 'col'), 0, 0, tiled=True)  32 us
    pallas_call x1, Pallas kernels, update(): pl.pallas_call(update_kernel, grid=(cols // QUARTER,), out_shape=jax.Shap...  25.9 us
    all_to_all x1, starting transfers between devices, relay(): held = lax.all_to_all(pieces, ('row', 'col'), 0, 0, tiled=True)  10.8 us
    unnamed x12, local copies, waits for them, and re-layouts  10.2 us
    pallas_call x1, Pallas kernels, solve_rows(): pl.pallas_call(solve_rows_kernel, grid=(rows // QUARTER,), out_shape=(jax...  6.93 us
    all_to_all x1, starting transfers between devices, relay(): back = lax.all_to_all(held, ('row', 'col'), 0, 0, tiled=True)  6.39 us
  transfers between devices with their start and end apart: 2, of which 2 were waited for; matrix products, arithmetic and copies ran while one was open for 1% of the time, Pallas kernels for 0%

profile of v2, /device:TPU:7, one launch (start us, length us, event | category | flops | bytes accessed | tf_op | source)
XLA Modules:
  0.0 254.5 jit_solution(14778851312838106641)
XLA Ops:
  0.6 1.9 copy.6
  2.6 1.8 pad.4
  4.4 10.8 %all-to-all-start = ((f32[128,5,8,128]{3,2,1,0:T(8,128)}), f32[128,5,8,128]{3,2,1,0:T(8,128)S(1)}, u32[]{:S(2)}, u32[]{:S(2)}) async-start(f32[128,5,8,128]{3,2,1,0:T(8,128)} %bitcast.31), calls=%async_computation | async-start | bytes 5242880 | tf_op jit(solution)/shard_map/all_to_all | solution.py:519
  15.2 0.7 gather_fusion.3
  15.9 0.7 gather_fusion.2
  16.6 0.1 fusion.1.index_ref
  16.7 32.6 %all-to-all-done.in_ref = f32[128,5,8,128]{3,2,1,0:T(8,128)S(1)} async-done(((f32[128,5,8,128]{3,2,1,0:T(8,128)}), f32[128,5,8,128]{3,2,1,0:T(8,128)S(1)}, u32[]{:S(2)}, u32[]{:S(2)}) %all-to-all-start) | async-done | bytes 2621472 | tf_op jit(solution)/shard_map/all_to_all | solution.py:519
  49.4 2.9 %reorder.1 = f32[128,5,8,128]{3,2,1,0:T(8,128)S(1)} custom-call(s32[128,5]{1,0:T(8,128)S(1)} %fusion.1.index_ref, f32[128,5,8,128]{3,2,1,0:T(8,128)S(1)} %all-to-all-done.in_ref), custom_call_target="tpu_custom_call" | custom-call | tf_op jit(solution)/shard_map/reorder/pallas_call | solution.py:505
  52.3 1.5 copy-done.3
  53.8 6.4 %all-to-all-start.1 = ((f32[128,5,8,128]{3,2,1,0:T(8,128)}), f32[128,5,8,128]{3,2,1,0:T(8,128)S(1)}, u32[]{:S(2)}, u32[]{:S(2)}) async-start(f32[128,5,8,128]{3,2,1,0:T(8,128)} %copy-done.3), calls=%async_computation.1 | async-start | bytes 5242880 | tf_op jit(solution)/shard_map/all_to_all | solution.py:527
  60.2 1.1 gather_fusion
  61.3 1.1 gather_fusion.1
  62.3 0.1 pad_add_fusion.1.place_ref
  62.5 32.0 %all-to-all-done.1 = f32[128,5,8,128]{3,2,1,0:T(8,128)S(1)} async-done(((f32[128,5,8,128]{3,2,1,0:T(8,128)}), f32[128,5,8,128]{3,2,1,0:T(8,128)S(1)}, u32[]{:S(2)}, u32[]{:S(2)}) %all-to-all-start.1) | async-done | bytes 2621472 | tf_op jit(solution)/shard_map/all_to_all | solution.py:527
  94.5 0.2 slice.20.items_ref
  94.6 3.4 %copy-done.4 = f32[1024,2048]{1,0:T(8,128)S(1)} copy-done((f32[1024,2048]{1,0:T(8,128)S(1)}, f32[1024,2048]{1,0:T(8,128)}, u32[]{:S(2)}) %copy-start.4) | copy-done | bytes 8388632
  98.0 1.6 assemble.1.front_ref
  99.6 0.1 slice.21.strip_ref
  99.7 3.1 %copy-done.2 = f32[1024,2048]{1,0:T(8,128)} copy-done((f32[1024,2048]{1,0:T(8,128)}, f32[1024,2048]{1,0:T(8,128)S(1)}, u32[]{:S(2)}) %copy-start.2) | copy-done | bytes 8388632
  102.8 0.1 slice.22.cols_ref
  102.9 116.5 %gather_factor.1 = (bf16[1024,1024]{1,0:T(8,128)(2,1)S(1)}, bf16[1024,1024]{1,0:T(8,128)(2,1)S(1)}, f32[1024,1024]{1,0:T(8,128)}, f32[8,128,2048]{2,1,0:T(8,128)}) custom-call(f32[1024,128]{1,0:T(8,128)S(1)} %slice.21.strip_ref, f32[128,2048]{1,0:T(8,128)S(1)} %slice.22.cols_ref), custom_call_target="tpu_custom_call" | custom-call | flops 49999998976 | bytes 8388608 | tf_op jit(solution)/shard_map/gather_factor/pallas_call | solution.py:401
  219.5 2.2 copy-done.5
  221.7 6.9 %solve_rows.1 = (f32[1024,1024]{1,0:T(8,128)}, bf16[1024,1024]{1,0:T(8,128)(2,1)S(1)}, bf16[1024,1024]{1,0:T(8,128)(2,1)S(1)}) custom-call(s32[2]{0:T(128)S(1)} %pad_add_fusion.1.place_ref, f32[1024,1024]{1,0:T(8,128)S(1)} %copy-done.5, bf16[1024,1024]{1,0:T(8,128)(2,1)S(1)} %get-tuple-element.10.xh_ref, bf16[1024,1024]{1,0:T(8,128)(2,1)S(1)} %get-tuple-element.11.xl_ref), custom_call_target="tpu_custom_call" | custom-call | tf_op jit(solution)/shard_map/solve_rows/pallas_call | solution.py:455
  228.6 25.9 %update.1 = f32[1024,2048]{1,0:T(8,128)} custom-call(f32[1024,2048]{1,0:T(8,128)} %copy-done.2, f32[8,128,2048]{2,1,0:T(8,128)} %get-tuple-element.9.w_ref, bf16[1024,1024]{1,0:T(8,128)(2,1)S(1)} %get-tuple-element.10.xh_ref, bf16[1024,1024]{1,0:T(8,128)(2,1)S(1)} %get-tuple-element.11.xl_ref, bf16[1024,1024]{1,0:T(8,128)(2,1)S(1)} %get-tuple-element.13.uh_ref, ...), custom_call_target="tpu_custom_call" | custom-call | tf_op jit(solution)/shard_map/update/pallas_call | solution.py:484
  (14 shorter events, 0.1 us)
Async XLA Ops:
  0.6 14.6 %copy-start = (s32[2,48]{1,0:T(2,128)S(1)}, s32[2,48]{1,0:T(2,128)}, u32[]{:S(2)}) copy-start(s32[2,48]{1,0:T(2,128)} %param.5) | copy-start | bytes 1156
  4.4 45.0 %all-to-all-start = ((f32[128,5,8,128]{3,2,1,0:T(8,128)}), f32[128,5,8,128]{3,2,1,0:T(8,128)S(1)}, u32[]{:S(2)}, u32[]{:S(2)}) async-start(f32[128,5,8,128]{3,2,1,0:T(8,128)} %bitcast.31), calls=%async_computation | async-start | bytes 5242880 | tf_op jit(solution)/shard_map/all_to_all | solution.py:519
  52.3 1.5 copy-start.3
  53.8 40.7 %all-to-all-start.1 = ((f32[128,5,8,128]{3,2,1,0:T(8,128)}), f32[128,5,8,128]{3,2,1,0:T(8,128)S(1)}, u32[]{:S(2)}, u32[]{:S(2)}) async-start(f32[128,5,8,128]{3,2,1,0:T(8,128)} %copy-done.3), calls=%async_computation.1 | async-start | bytes 5242880 | tf_op jit(solution)/shard_map/all_to_all | solution.py:527
  94.6 3.4 %copy-start.4 = (f32[1024,2048]{1,0:T(8,128)S(1)}, f32[1024,2048]{1,0:T(8,128)}, u32[]{:S(2)}) copy-start(f32[1024,2048]{1,0:T(8,128)} %front_ref.1) | copy-start | bytes 25165828
  99.6 3.2 %copy-start.2 = (f32[1024,2048]{1,0:T(8,128)}, f32[1024,2048]{1,0:T(8,128)S(1)}, u32[]{:S(2)}) copy-start(f32[1024,2048]{1,0:T(8,128)S(1)} %assemble.1.front_ref) | copy-start | bytes 25165828
  219.5 2.2 copy-start.5
  228.6 25.9 %copy-start.1 = (s32[2,48]{1,0:T(2,128)S(1)}, s32[2,48]{1,0:T(2,128)}, u32[]{:S(2)}) copy-start(s32[2,48]{1,0:T(2,128)} %param.5) | copy-start | bytes 1156

commit v3 on v2

--- a/solution.py
+++ b/solution.py
@@ -12,9 +12,9 @@
 PIVOTS = 1024
 STEPS = PIVOTS // TILE
 SUB = 8
+STRIDE1 = 29
+STRIDE2 = 37
 GROUPS = TILE // SUB
-ITEMS = 36
-SHARE = 5
 MIB = 2**20
 
 
@@ -189,7 +189,90 @@
         guarded(guard, wait)
 
 
-def gather_kernel(strip_ref, cols_ref, xh_ref, xl_ref, wrow_ref, wcol_ref, pivots, work, send_sems, recv_sems):
+def relay(r, c, rows, cols, map_ref, child_ref, moved_ref, held, turned, sems):
+    groups = 2 * 3
+    me = r * cols + c
+    group = (c + cols - 2 * r % cols) % cols
+    holds = group < groups
+    child, run = group // 3 % 2, group % 3
+    count = rows * groups
+
+    def column(k, g):
+        return (g + 2 * k) % cols
+
+    def rows_of(g, k):
+        return pl.ds(pl.multiple_of(g % 3 * TILE + k * SUB, SUB), SUB)
+
+    def first(k, g):
+        return pltpu.make_async_remote_copy(
+            src_ref=child_ref.at[g // 3, rows_of(g, k)],
+            dst_ref=held.at[me],
+            send_sem=sems.at[0],
+            recv_sem=sems.at[1],
+            device_id=(k, column(k, g)),
+            device_id_type=pl.DeviceIdType.MESH,
+        )
+
+    def second(e):
+        return pltpu.make_async_remote_copy(
+            src_ref=turned.at[e],
+            dst_ref=moved_ref.at[child, rows_of(group, r)],
+            send_sem=sems.at[2],
+            recv_sem=sems.at[3],
+            device_id=(e // cols, e % cols),
+            device_id_type=pl.DeviceIdType.MESH,
+        )
+
+    def all_of(ref, n):
+        return ref.at[pl.ds(0, n)]
+
+    def waiting(n, sem):
+        return pltpu.make_async_copy(all_of(held, n), all_of(turned, n), sem)
+
+    @pl.loop(0, count)
+    def _(i):
+        j = i * STRIDE1 % count
+        k, g = (r + j // groups) % rows, (j + c) % groups
+
+        @pl.when(k * cols + column(k, g) != me)
+        def _():
+            first(k, g).start()
+
+    @pl.when(holds)
+    def _():
+        held[me] = child_ref[child, rows_of(group, r)]
+        waiting(rows * cols - 1, sems.at[1]).wait()
+        row_start = map_ref[child, run * RUN]
+        col_starts = [map_ref[child, n * RUN] for n in range(3)]
+
+        @pl.loop(0, rows * cols)
+        def _(i):
+            e = (me + i * STRIDE2) % (rows * cols)
+            source = (e // cols + 2 * TILE - row_start) % rows * cols
+            for n in range(3):
+                part = slice(n * 2 * TILE, (n + 1) * 2 * TILE)
+                turned[e, :, part] = held[source + (e % cols + 2 * TILE - col_starts[n]) % cols, :, part]
+
+            @pl.when(i > 0)
+            def _():
+                second(e).start()
+
+        moved_ref[child, rows_of(group, r)] = turned[me]
+        waiting(count - 1, sems.at[0]).wait()
+        waiting(rows * cols - 1, sems.at[2]).wait()
+        waiting(count - 1, sems.at[3]).wait()
+
+    @pl.when(group >= groups)
+    def _():
+        waiting(count, sems.at[0]).wait()
+        waiting(count, sems.at[3]).wait()
+
+
+def gather_kernel(
+    map_ref, strip_ref, cols_ref, child_ref, xh_ref, xl_ref, wrow_ref, wcol_ref, moved_ref,
+    held, turned, pivots, work, relay_sems, send_sems, recv_sems,
+):
+    rows, cols = lax.axis_size("row"), lax.axis_size("col")
     r, c = lax.axis_index("row"), lax.axis_index("col")
     x, yl, core = r // 4, r // 2 % 2, r % 2
     yh, z = c // 4, c % 4
@@ -205,20 +288,47 @@
         return (at[dim] + step) % 4
 
     barrier = pltpu.get_barrier_semaphore()
-    for dim in "xyz":
-        for step in range(1, 4):
-            pl.semaphore_signal(
-                barrier, inc=1, device_id=device(**{dim: moved(dim, step)}), device_id_type=pl.DeviceIdType.MESH
-            )
-    pl.semaphore_signal(barrier, inc=1, device_id=device(core=1 - core), device_id_type=pl.DeviceIdType.MESH)
+
+    @pl.loop(1, rows * cols)
+    def _(i):
+        e = (r * cols + c + i) % (rows * cols)
+        pl.semaphore_signal(barrier, inc=1, device_id=(e // cols, e % cols), device_id_type=pl.DeviceIdType.MESH)
+
+    pl.semaphore_wait(barrier, rows * cols - 1)
+    relay(r, c, rows, cols, map_ref, child_ref, moved_ref, held, turned, relay_sems)
+
+    def kept(condition, value):
+        return jnp.where(condition, value, jnp.zeros_like(value))
+
+    own_cols = pl.ds(pl.multiple_of(c * TILE, TILE), TILE)
+    for slot in range(rows // 2):
+        block = slice(slot * TILE, (slot + 1) * TILE)
+        total = strip_ref[block, :]
+        for child in range(2):
+            inside = c >= map_ref[child, 0]
+            for run in range(3):
+                offset = slot * rows + r - map_ref[child, run * RUN]
+                total = total + kept(
+                    inside & (offset >= 0) & (offset < RUN), moved_ref[child, run * TILE : (run + 1) * TILE, :TILE]
+                )
+        wrow_ref[block, own_cols] = total
 
     @pl.when(near)
     def _():
-        pivots[core, xs, y, z] = strip_ref[:TILE, :]
-        wcol_ref[r % 8] = cols_ref[...]
-
-    wrow_ref[:, pl.ds(pl.multiple_of(c * TILE, TILE), TILE)] = strip_ref[...]
-    pl.semaphore_wait(barrier, 10)
+        pivots[core, xs, y, z] = wrow_ref[:TILE, own_cols]
+        for slot in range(2 * cols):
+            block = slice(slot * TILE, (slot + 1) * TILE)
+            total = cols_ref[:, block]
+            for child in range(2):
+                inside = r >= map_ref[child, 0]
+                for tile in range(6):
+                    offset = slot * cols + c - map_ref[child, tile // 2 * RUN] - tile % 2 * cols
+                    total = total + kept(
+                        inside & (offset >= 0) & (offset < cols),
+                        moved_ref[child, :TILE, tile * TILE : (tile + 1) * TILE],
+                    )
+            wcol_ref[r % 8, :, block] = total
+
     ex = Exchange(send_sems, recv_sems)
 
     def pivot_phase(rows, order, number):
@@ -258,146 +368,127 @@
 
         return begin([ex.copy(pivots, block(core), block(1 - core), device(core=1 - core))])
 
+    def tiles(first, count):
+        return pl.ds(pl.multiple_of(first * TILE, TILE), count * TILE)
+
+    def panel_row(rows, first, count, first_in, device):
+        return ex.copy(wrow_ref, (rows, tiles(first, count)), (rows, tiles(first_in, count)), device)
+
+    def panel_col(chunk, out, into, device, sends=None, receives=None):
+        return ex.copy(
+            wcol_ref, (out, pl.ds(0, TILE), chunk), (into, pl.ds(0, TILE), chunk), device, sends, receives
+        )
+
+    def owner(x, yl, core=core):
+        return x * 4 + yl * 2 + core
+
+    y_far = device(y=(y + 2) % 4)
+    y_pair = device(y=yh * 2 + 1 - yl)
+    x_pair = device(x=(5 - x) % 4)
+    sibling = device(core=1 - core)
+    top, bottom = pl.ds(0, ROW_SPLIT), pl.ds(ROW_SPLIT, strip_ref.shape[0] - ROW_SPLIT)
+    top_first = [panel_row(top, c, 1, (c + cols // 2) % cols, y_far)]
+    bottom_first = [
+        panel_row(bottom, c, 1, yh * 4 + moved("z", -step), device(z=moved("z", step))) for step in range(1, 4)
+    ]
+    top_last = [
+        panel_row(top, h * 4 + z, 1, h * 4 + moved("z", -step), device(z=moved("z", step)))
+        for step in (1, 3, 2)
+        for h in range(2)
+    ]
+    bottom_last = [panel_row(bottom, yh * 4, 4, (1 - yh) * 4, y_far)]
+
+    def beside(chunk, halves):
+        return [
+            panel_col(
+                chunk,
+                owner(xs, h),
+                owner(moved("x", -step) % 2, h),
+                device(x=moved("x", step)),
+                near,
+                moved("x", -step) < 2,
+            )
+            for step in (1, 3)
+            for h in halves
+        ]
+
+    def onward(chunk, halves):
+        far = x >= 2
+        return [panel_col(chunk, owner((x + 1) % 2, h), owner(xs, h), x_pair, far, far) for h in halves]
+
+    def swapped(chunk):
+        return [
+            panel_col(chunk, owner(a, b), owner(a, b, 1 - core), sibling) for a in range(2) for b in range(2)
+        ]
+
+    chunks = [pl.ds(TILE + n * 5 * TILE, 5 * TILE) for n in range(3)]
+    both = (0, 1)
+    a_x, a_on = beside(chunks[0], (yl,)), onward(chunks[0], (yl,))
+    a_y = [panel_col(chunks[0], owner(h, yl), owner(h, 1 - yl), y_pair) for h in both]
+    b_y, c_y = ([panel_col(chunks[n], owner(xs, yl), owner(xs, 1 - yl), y_pair, near, near)] for n in (1, 2))
+    b_x, c_x = (beside(chunks[n], both) for n in (1, 2))
+    b_on, c_on = (onward(chunks[n], both) for n in (1, 2))
+    swaps = [swapped(chunk) for chunk in chunks]
+
     parts = (((0, 48), "xyz"), ((48, 96), "zxy"), ((96, 128), "yzx"))
     pending = [pivot_phase(rows, order, 0) for rows, order in parts]
     for number in (1, 2):
         for p, (rows, order) in enumerate(parts):
             finish(pending[p])
             pending[p] = pivot_phase(rows, order, number)
+        if number == EARLY:
+            for copies in (a_x, b_y, bottom_first, c_y, top_first):
+                begin(copies)
     for p, (rows, order) in enumerate(parts):
         finish(pending[p])
         pending[p] = pivot_swap(rows)
-
-    low, high = (pl.ds(0, 512), pl.ds(512, 512))
-    left, right = (pl.ds(0, 1024), pl.ds(1024, 1024))
-
-    def tiles(first, count):
-        return pl.ds(pl.multiple_of(first * TILE, TILE), count * TILE)
-
-    def owner(x, yl):
-        return x * 4 + yl * 2 + core
-
-    first_row = [ex.copy(wrow_ref, (low, tiles(c, 1)), (low, tiles((c + 4) % 8, 1)), device(y=(y + 2) % 4))]
-    second_row = [
-        ex.copy(
-            wrow_ref,
-            (high, tiles(c, 1)),
-            (high, tiles(yh * 4 + moved("z", -step), 1)),
-            device(z=moved("z", step)),
-        )
-        for step in range(1, 4)
-    ]
-    first_col = [
-        ex.copy(
-            wcol_ref,
-            (owner(xs, yl), pl.ds(0, TILE), left),
-            (owner(moved("x", -step) % 2, yl), pl.ds(0, TILE), left),
-            device(x=moved("x", step)),
-            near,
-            moved("x", -step) < 2,
-        )
-        for step in range(1, 4)
-    ]
-    y_pair = yh * 2 + 1 - yl
-    second_col = [
-        ex.copy(
-            wcol_ref,
-            (owner(xs, yl), pl.ds(0, TILE), right),
-            (owner(xs, 1 - yl), pl.ds(0, TILE), right),
-            device(y=y_pair),
-            near,
-            near,
-        )
-    ]
-    for copies in (first_row, second_row, first_col, second_col):
-        begin(copies)
     for p in range(3):
         finish(pending[p])
     load_block(pivots, work)
-    last_row = [
-        ex.copy(
-            wrow_ref,
-            (low, tiles(h * 4 + z, 1)),
-            (low, tiles(h * 4 + moved("z", -step), 1)),
-            device(z=moved("z", step)),
-        )
-        for step in range(1, 4)
-        for h in range(2)
-    ]
-    side_row = [ex.copy(wrow_ref, (high, tiles(yh * 4, 4)), (high, tiles((1 - yh) * 4, 4)), device(y=(y + 2) % 4))]
-    far_col = [
-        ex.copy(
-            wcol_ref,
-            (owner(xs, h), pl.ds(0, TILE), right),
-            (owner(moved("x", -step) % 2, h), pl.ds(0, TILE), right),
-            device(x=moved("x", step)),
-            near,
-            moved("x", -step) < 2,
-        )
-        for step in range(1, 4)
-        for h in range(2)
-    ]
-    side_col = [
-        ex.copy(wcol_ref, (owner(h, yl), pl.ds(0, TILE), left), (owner(h, 1 - yl), pl.ds(0, TILE), left), device(y=y_pair))
-        for h in range(2)
-    ]
-    swaps = [
-        [
-            ex.copy(
-                wcol_ref,
-                (4 * a + 2 * b + core, pl.ds(0, TILE), half),
-                (4 * a + 2 * b + 1 - core, pl.ds(0, TILE), half),
-                device(core=1 - core),
-            )
-            for a in range(2)
-            for b in range(2)
-        ]
-        for half in (left, right)
-    ]
-
-    def middle():
-        finish(first_row)
-        begin(last_row)
-        finish(second_row)
-        begin(side_row)
-        finish(second_col)
-        begin(far_col)
-        finish(first_col)
-        begin(side_col)
-
-    def swap_cols():
-        for copies, swap in ((side_col, swaps[0]), (far_col, swaps[1])):
-            finish(copies)
-            begin(swap)
+
+    def then(before, after):
+        finish(before)
+        begin(after)
+
+    plan = {
+        1: [(a_x, a_on)],
+        2: [(b_y, b_x), (top_first, top_last)],
+        3: [(a_on, a_y), (bottom_first, bottom_last)],
+        4: [(c_y, c_x)],
+        5: [(b_x, b_on)],
+        6: [(a_y, swaps[0])],
+        7: [(c_x, c_on)],
+    }
 
     def between(k):
-        pl.when(k == 3)(middle)
-        pl.when(k == 6)(swap_cols)
-
-    if OVERLAP:
-        factor_steps(work, between)
-    else:
-        middle()
-        swap_cols()
-        factor_steps(work, lambda k: None)
-    finish(last_row)
-    finish(side_row)
-    finish(swaps[0])
-    finish(swaps[1])
+        for step, pairs in plan.items():
+
+            @pl.when(k == step)
+            def _():
+                for before, after in pairs:
+                    then(before, after)
+
+    factor_steps(work, between)
+    then(b_on, swaps[1])
+    then(c_on, swaps[2])
+    for copies in (top_last, bottom_last, *swaps):
+        finish(copies)
     ex.drain()
     for i in range(STEPS):
         rows = slice(i * TILE, (i + 1) * TILE)
         xh_ref[rows], xl_ref[rows] = split2(work[rows, PIVOTS:])
 
 
-OVERLAP = True
+ROW_SPLIT = 768
+EARLY = 2
 COPIES = 80
 
 
-def gather_and_factor(row_strip, col_strip):
+def gather_and_factor(child_map, row_strip, col_strip, children):
     vmem = pl.BlockSpec(memory_space=pltpu.VMEM)
     local_rows, local_cols = row_strip.shape[0], col_strip.shape[1]
     half = jax.ShapeDtypeStruct((PIVOTS, PIVOTS), bf16)
+    slices = (lax.axis_size("row") * lax.axis_size("col"), SUB, children.shape[2])
     return pl.pallas_call(
         gather_kernel,
         out_shape=(
@@ -405,21 +496,25 @@
             half,
             jax.ShapeDtypeStruct((local_rows, PIVOTS), f32),
             jax.ShapeDtypeStruct((STEPS, TILE, local_cols), f32),
+            jax.ShapeDtypeStruct(children.shape, f32),
         ),
-        in_specs=[vmem] * 2,
-        out_specs=(vmem,) * 4,
+        in_specs=[pl.BlockSpec(memory_space=pltpu.SMEM)] + [vmem] * 3,
+        out_specs=(vmem,) * 5,
         scratch_shapes=[
+            pltpu.VMEM(slices, f32),
+            pltpu.VMEM(slices, f32),
             pltpu.VMEM((2, 2, 4, 4, TILE, TILE), f32),
             pltpu.VMEM((PIVOTS, 2 * PIVOTS), f32),
+            pltpu.SemaphoreType.DMA((4,)),
             pltpu.SemaphoreType.DMA((COPIES,)),
             pltpu.SemaphoreType.DMA((COPIES,)),
         ],
         compiler_params=pltpu.CompilerParams(
-            vmem_limit_bytes=48 * MIB, collective_id=0, has_side_effects=True
+            vmem_limit_bytes=56 * MIB, collective_id=0, has_side_effects=True
         ),
         cost_estimate=pl.CostEstimate(flops=5 * 10**10, bytes_accessed=8 * MIB, transcendentals=0),
         name="gather_factor",
-    )(row_strip, col_strip)
+    )(child_map, row_strip, col_strip, children)
 
 
 def dot3(ah, al, bh, bl, dims):
@@ -463,7 +558,7 @@
     )(place, panel, xh, xl)
 
 
-def update_kernel(front_ref, w_ref, xh_ref, xl_ref, uh_ref, ul_ref, out_ref, bh, bl):
+def update_kernel(slots_ref, front_ref, moved_ref, w_ref, xh_ref, xl_ref, uh_ref, ul_ref, out_ref, bh, bl):
     wh, wl = split2(w_ref[...].reshape(PIVOTS, QUARTER))
     for n in range(PIVOTS // QUARTER):
         block = slice(n * QUARTER, (n + 1) * QUARTER)
@@ -474,9 +569,19 @@
     for n in range(front_ref.shape[0] // QUARTER):
         block = slice(n * QUARTER, (n + 1) * QUARTER)
         out_ref[block] = front_ref[block] - dot3(uh_ref[block], ul_ref[block], bh[...], bl[...], ((1,), (0,)))
-
-
-def update(front, panel, xh, xl, uh, ul):
+    for child in range(2):
+        for tile in range(6):
+            slot = slots_ref[1, child * 6 + tile]
+
+            @pl.when(slot // (QUARTER // TILE) == pl.program_id(0))
+            def _():
+                col = pl.ds(pl.multiple_of(slot % (QUARTER // TILE) * TILE, TILE), TILE)
+                for run in range(3):
+                    row = pl.ds(pl.multiple_of(slots_ref[0, child * 3 + run] * TILE, TILE), TILE)
+                    out_ref[row, col] += moved_ref[child, run * TILE : (run + 1) * TILE, tile * TILE : (tile + 1) * TILE]
+
+
+def update(slots, front, moved, panel, xh, xl, uh, ul):
     rows, cols = front.shape
     whole = pl.BlockSpec((PIVOTS, PIVOTS), lambda j: (0, 0))
     rows_whole = pl.BlockSpec((rows, PIVOTS), lambda j: (0, 0))
@@ -485,86 +590,35 @@
         update_kernel,
         grid=(cols // QUARTER,),
         out_shape=jax.ShapeDtypeStruct(front.shape, f32),
-        in_specs=[block, pl.BlockSpec((STEPS, TILE, QUARTER), lambda j: (0, 0, j)), whole, whole, rows_whole, rows_whole],
+        in_specs=[
+            pl.BlockSpec(memory_space=pltpu.SMEM),
+            block,
+            pl.BlockSpec(moved.shape, lambda j: (0, 0, 0)),
+            pl.BlockSpec((STEPS, TILE, QUARTER), lambda j: (0, 0, j)),
+            whole,
+            whole,
+            rows_whole,
+            rows_whole,
+        ],
         out_specs=block,
         scratch_shapes=[pltpu.VMEM((PIVOTS, QUARTER), bf16)] * 2,
         compiler_params=pltpu.CompilerParams(vmem_limit_bytes=40 * MIB),
         name="update",
-    )(front, panel, xh, xl, uh, ul)
-
-
-def reorder_kernel(index_ref, in_ref, out_ref):
-    @pl.loop(0, in_ref.shape[0])
-    def _(d):
-        for m in range(SHARE):
-            out_ref[d, m] = in_ref[index_ref[d, m], m]
-
-
-def reorder(pieces, index):
-    vmem = pl.BlockSpec(memory_space=pltpu.VMEM)
-    return pl.pallas_call(
-        reorder_kernel,
-        out_shape=jax.ShapeDtypeStruct(pieces.shape, f32),
-        in_specs=[pl.BlockSpec(memory_space=pltpu.SMEM), vmem],
-        out_specs=vmem,
-        compiler_params=pltpu.CompilerParams(vmem_limit_bytes=16 * MIB),
-        name="reorder",
-    )(index, pieces)
-
-
-def relay(children, child_map, rows, cols, row_index, col_index):
-    pieces = children.reshape(2, 3, rows, SUB, 6, TILE).transpose(2, 0, 1, 4, 3, 5).reshape(rows, ITEMS, SUB, TILE)
-    pieces = jnp.pad(pieces, ((0, 0), (0, cols * SHARE - ITEMS), (0, 0), (0, 0)))
-    pieces = pieces.reshape(rows * cols, SHARE, SUB, TILE)
-    held = lax.all_to_all(pieces, ("row", "col"), 0, 0, tiled=True)
-    item = jnp.minimum(col_index * SHARE + jnp.arange(SHARE), ITEMS - 1)
-    child, run, tile = item // 18, item % 18 // 6, item % 6
-    row_start = child_map[child, run * RUN]
-    col_start = child_map[child, tile // 2 * RUN]
-    target = jnp.arange(rows * cols, dtype=jnp.int32)[:, None]
-    index = (target // cols - row_start) % rows * cols + (target % cols - col_start) % cols
-    held = reorder(held, index.astype(jnp.int32))
-    back = lax.all_to_all(held, ("row", "col"), 0, 0, tiled=True)
-    return back.reshape(rows, cols * SHARE, SUB, TILE)[:, :ITEMS]
-
-
-def assemble_kernel(slots_ref, front_ref, items_ref, out_ref):
-    out_ref[...] = front_ref[...]
-    for m in range(ITEMS):
-        row = pl.ds(pl.multiple_of(slots_ref[0, m] * TILE, TILE), TILE)
-        col = pl.ds(pl.multiple_of(slots_ref[1, m] * TILE, TILE), TILE)
-        out_ref[row, col] += items_ref[:, m].reshape(TILE, TILE)
-
-
-def assemble(front, items, child_map, rows, cols, row_index, col_index):
-    item = jnp.arange(ITEMS)
-    child, run, tile = item // 18, item % 18 // 6, item % 6
-    row_start = child_map[child, run * RUN]
-    col_start = child_map[child, tile // 2 * RUN]
-    row_slot = (row_start + (row_index - row_start) % rows) // rows
-    col_slot = (col_start + (col_index - col_start) % cols) // cols + tile % 2
-    slots = jnp.stack([row_slot, col_slot]).astype(jnp.int32)
-    vmem = pl.BlockSpec(memory_space=pltpu.VMEM)
-    return pl.pallas_call(
-        assemble_kernel,
-        out_shape=jax.ShapeDtypeStruct(front.shape, f32),
-        in_specs=[pl.BlockSpec(memory_space=pltpu.SMEM), vmem, vmem],
-        out_specs=vmem,
-        compiler_params=pltpu.CompilerParams(vmem_limit_bytes=32 * MIB),
-        name="assemble",
-    )(slots, front, items)
+    )(slots, front, moved, panel, xh, xl, uh, ul)
 
 
 def per_device(front, children, child_map):
     rows, cols = lax.axis_size("row"), lax.axis_size("col")
     row_index, col_index = lax.axis_index("row"), lax.axis_index("col")
-    local_rows, local_cols = front.shape
-    items = relay(children, child_map, rows, cols, row_index, col_index)
-    assembled = assemble(front, items, child_map, rows, cols, row_index, col_index)
-    xh, xl, row_panel, col_panel = gather_and_factor(assembled[:, :TILE], assembled[:TILE, :])
+    xh, xl, row_panel, col_panel, moved = gather_and_factor(child_map, front[:, :TILE], front[:TILE, :], children)
     place = jnp.stack([jnp.int32(rows), row_index])
     lower_panel, uh, ul = solve_rows(place, row_panel, xh, xl)
-    front_out = update(assembled, col_panel, xh, xl, uh, ul)
+    starts = child_map[:, ::RUN]
+    row_slots = (starts + (row_index - starts) % rows) // rows
+    col_slots = (starts + (col_index - starts) % cols) // cols
+    col_slots = col_slots[:, :, None] + jnp.arange(RUN // cols)[None, None, :]
+    slots = jnp.zeros((2, 12), jnp.int32).at[0, :6].set(row_slots.reshape(-1)).at[1].set(col_slots.reshape(-1))
+    front_out = update(slots, front, moved, col_panel, xh, xl, uh, ul)
     return front_out, lower_panel
 
 

time: 255 us -> 239 us (0.937)
  Pallas kernels: 154 us -> 228 us
  waiting for transfers between devices: 64.6 us -> 0 us
  starting transfers between devices: 17.2 us -> 0 us
  local copies, waits for them, and re-layouts: 17.7 us -> 10.5 us
    pallas_call x1, Pallas kernels: 117 us -> 194 us  [gather_and_factor(): pl.pallas_call(gather_kernel, out_shape=(half, half, jax.ShapeDtypeStruct...]
    all_to_all x2 -> x0, waiting for transfers between devices: 64.6 us -> none  [the longest x1 32.6 us: relay(): held = lax.all_to_all(pieces, ('row', 'col'), 0, 0, tiled=True)]
    all_to_all x2 -> x0, starting transfers between devices: 17.2 us -> none  [the longest x1 10.8 us: relay(): held = lax.all_to_all(pieces, ('row', 'col'), 0, 0, tiled=True)]
    unnamed x12 -> x8, local copies, waits for them, and re-layouts: 10.2 us -> 5.37 us
    slice x3, local copies, waits for them, and re-layouts: 0.32 us -> 4.93 us  [the longest x1 2.29 us: per_device(): front[:TILE, :]]
    pallas_call x2 -> x0, Pallas kernels: 4.49 us -> none  [the longest x1 2.89 us: reorder(): pl.pallas_call(reorder_kernel, out_shape=jax.ShapeDtypeStruct(pieces.shap...]
    gather x4 -> x0, local copies, waits for them, and re-layouts: 3.47 us -> none  [the longest x1 1.06 us: assemble(): col_start = child_map[child, tile // 2 * RUN]]
  transfers between devices with their start and end apart: 2 -> 0, of which waited for: 2 -> 0; matrix products, arithmetic and copies ran while one was open for 1% -> 0% of each run, Pallas kernels for 0% -> 0%
where the time goes in v3:
time: 239 us
  Pallas kernels  228 us (95%)
  local copies, waits for them, and re-layouts  10.5 us (4%)
    pallas_call x1, Pallas kernels, gather_and_factor(): pl.pallas_call(gather_kernel, out_shape=(half, half, jax.ShapeDtypeStruct...  194 us
    pallas_call x1, Pallas kernels, update(): pl.pallas_call(update_kernel, grid=(cols // QUARTER,), out_shape=jax.Shap...  27.1 us
    pallas_call x1, Pallas kernels, solve_rows(): pl.pallas_call(solve_rows_kernel, grid=(rows // QUARTER,), out_shape=(jax...  6.87 us
    unnamed x8, local copies, waits for them, and re-layouts  5.37 us

profile of v3, /device:TPU:7, one launch (start us, length us, event | category | flops | bytes accessed | tf_op | source)
XLA Modules:
  0.0 238.9 jit_solution(8067948807739075114)
XLA Ops:
  0.6 0.1 pad_add_fusion.place_ref
  0.7 0.8 slice.40
  1.5 0.1 reshape.84
  1.6 0.1 iota_add_fusion
  1.7 0.1 add.54
  1.8 1.9 slice.41.strip_ref
  3.7 2.3 slice.42.cols_ref
  6.0 193.6 %gather_factor.1 = (bf16[1024,1024]{1,0:T(8,128)(2,1)}, bf16[1024,1024]{1,0:T(8,128)(2,1)}, f32[1024,1024]{1,0:T(8,128)}, f32[8,128,2048]{2,1,0:T(8,128)}, f32[2,384,768]{2,1,0:T(8,128)}) custom-call(s32[2,48]{1,0:T(2,128)} %map_ref.1, f32[1024,128]{1,0:T(8,128)} %slice.41.strip_ref, f32[128,2048]{1,0:T(8,128)} %slice.42.cols_ref, f32[2,384,768]{2,1,0:T(8,128)} %child_ref.1), custom_call_target="tpu_custom_call" | custom-call | flops 49999998976 | bytes 8388608 | tf_op jit(solution)/shard_map/gather_factor/pallas_call | solution.py:492
  199.5 0.0 copy-start
  199.5 1.6 copy-done
  201.1 0.0 copy-start.1
  201.1 1.6 copy-done.1
  202.7 0.0 copy-start.2
  202.7 2.2 copy-done.2
  204.9 0.0 copy-start.3
  204.9 6.9 %solve_rows.1 = (f32[1024,1024]{1,0:T(8,128)}, bf16[1024,1024]{1,0:T(8,128)(2,1)S(1)}, bf16[1024,1024]{1,0:T(8,128)(2,1)S(1)}) custom-call(s32[2]{0:T(128)S(1)} %pad_add_fusion.place_ref, f32[1024,1024]{1,0:T(8,128)S(1)} %copy-done.2, bf16[1024,1024]{1,0:T(8,128)(2,1)S(1)} %copy-done, bf16[1024,1024]{1,0:T(8,128)(2,1)S(1)} %copy-done.1), custom_call_target="tpu_custom_call" | custom-call | tf_op jit(solution)/shard_map/solve_rows/pallas_call | solution.py:550
  211.8 0.0 copy-done.3
  211.8 27.1 %update.1 = f32[1024,2048]{1,0:T(8,128)} custom-call(s32[2,12]{1,0:T(2,128)S(1)} %scatter.9.slots_ref, f32[1024,2048]{1,0:T(8,128)} %front_ref.1, f32[2,384,768]{2,1,0:T(8,128)S(1)} %copy-done.3, f32[8,128,2048]{2,1,0:T(8,128)} %get-tuple-element.35.w_ref, bf16[1024,1024]{1,0:T(8,128)(2,1)S(1)} %copy-done, bf16[1024,1024]{1,0:T(8,128)(2,1)S(1)} %copy-done.1, ...), custom_call_target="tpu_custom_call" | custom-call | tf_op jit(solution)/shard_map/update/pallas_call | solution.py:589
  (3 shorter events, 0.1 us)
Async XLA Ops:
  199.5 1.6 copy-start
  201.1 1.6 copy-start.1
  202.7 2.2 copy-start.2
  204.9 6.9 %copy-start.3 = (f32[2,384,768]{2,1,0:T(8,128)S(1)}, f32[2,384,768]{2,1,0:T(8,128)}, u32[]{:S(2)}) copy-start(f32[2,384,768]{2,1,0:T(8,128)} %get-tuple-element.34.moved_ref) | copy-start | bytes 7077892

commit v4 on v3

--- a/solution.py
+++ b/solution.py
@@ -118,7 +118,7 @@
 
     @pl.loop(0, STEPS)
     def _(k):
-        between(k)
+        between(k, 0)
         kb = pl.ds(pl.multiple_of(k * TILE, TILE), TILE)
         window = pl.ds(pl.multiple_of(k * TILE, TILE), width)
         tile = work[kb, kb]
@@ -127,6 +127,7 @@
         a = [tile[SUB * i : SUB * i + SUB] for i in range(GROUPS)]
         e = [(ri + SUB * i == ci).astype(f32) for i in range(GROUPS)]
         inverse = factor_tile(a, e)
+        between(k, 1)
         work[kb, window] = mm3(inverse, work[kb, window], ((1,), (0,)))
 
         @pl.loop(k + 1, STEPS)
@@ -163,12 +164,15 @@
         def wait_send():
             made(out_at, ref.at[out_at] if source is None else source).wait_send()
 
-        self.sent.append((sends, wait_send))
-        return (sends, start), (receives, wait_recv)
-
-    def drain(self):
-        for guard, wait in self.sent:
+        sent = (sends, wait_send)
+        self.sent.append(sent)
+        return (sends, start), (receives, wait_recv), sent
+
+    def drain(self, copies=None):
+        waits = self.sent if copies is None else [copy[2] for copy in copies]
+        for guard, wait in waits:
             guarded(guard, wait)
+        self.sent = [w for w in self.sent if not any(w is done for done in waits)]
 
 
 def guarded(guard, action):
@@ -179,13 +183,13 @@
 
 
 def begin(copies):
-    for (guard, start), _ in copies:
+    for (guard, start), _, _ in copies:
         guarded(guard, start)
     return copies
 
 
 def finish(copies):
-    for _, (guard, wait) in copies:
+    for _, (guard, wait), _ in copies:
         guarded(guard, wait)
 
 
@@ -269,8 +273,10 @@
 
 
 def gather_kernel(
-    map_ref, strip_ref, cols_ref, child_ref, xh_ref, xl_ref, wrow_ref, wcol_ref, moved_ref,
-    held, turned, pivots, work, relay_sems, send_sems, recv_sems,
+    map_ref, front_ref, child_ref, solved_out, uh_out, ul_out, bh_out, bl_out, moved_out,
+    wrow_ref, uh_ref, ul_ref, bh_ref, bl_ref, moved_ref,
+    strip_ref, cols_ref, xh_ref, xl_ref, wcol_ref, held, turned, pivots, work,
+    strip_sems, out_sems, relay_sems, send_sems, recv_sems,
 ):
     rows, cols = lax.axis_size("row"), lax.axis_size("col")
     r, c = lax.axis_index("row"), lax.axis_index("col")
@@ -287,6 +293,12 @@
     def moved(dim, step):
         return (at[dim] + step) % 4
 
+    strips = [
+        pltpu.make_async_copy(front_ref.at[:, pl.ds(0, TILE)], strip_ref, strip_sems.at[0]),
+        pltpu.make_async_copy(front_ref.at[pl.ds(0, TILE), :], cols_ref, strip_sems.at[1]),
+    ]
+    for copy in strips:
+        copy.start()
     barrier = pltpu.get_barrier_semaphore()
 
     @pl.loop(1, rows * cols)
@@ -296,6 +308,17 @@
 
     pl.semaphore_wait(barrier, rows * cols - 1)
     relay(r, c, rows, cols, map_ref, child_ref, moved_ref, held, turned, relay_sems)
+
+    results = []
+
+    def deliver(src, dst):
+        copy = pltpu.make_async_copy(src, dst, out_sems.at[len(results)])
+        copy.start()
+        results.append(copy)
+
+    deliver(moved_ref, moved_out)
+    for copy in strips:
+        copy.wait()
 
     def kept(condition, value):
         return jnp.where(condition, value, jnp.zeros_like(value))
@@ -437,7 +460,7 @@
             finish(pending[p])
             pending[p] = pivot_phase(rows, order, number)
         if number == EARLY:
-            for copies in (a_x, b_y, bottom_first, c_y, top_first):
+            for copies in (a_x, b_y, bottom_first, top_first, c_y):
                 begin(copies)
     for p, (rows, order) in enumerate(parts):
         finish(pending[p])
@@ -451,32 +474,83 @@
         begin(after)
 
     plan = {
-        1: [(a_x, a_on)],
-        2: [(b_y, b_x), (top_first, top_last)],
-        3: [(a_on, a_y), (bottom_first, bottom_last)],
-        4: [(c_y, c_x)],
-        5: [(b_x, b_on)],
-        6: [(a_y, swaps[0])],
-        7: [(c_x, c_on)],
+        (0, 0): [(a_x, a_on), (b_y, b_x)],
+        (0, 1): [(top_first, top_last)],
+        (1, 1): [(a_on, a_y), (bottom_first, bottom_last)],
+        (2, 0): [(c_y, c_x)],
+        (2, 1): [(b_x, b_on)],
+        (5, 0): [(c_x, c_on), (b_on, swaps[1])],
+        (4, 1): [(a_y, swaps[0])],
     }
 
-    def between(k):
-        for step, pairs in plan.items():
-
-            @pl.when(k == step)
-            def _():
-                for before, after in pairs:
-                    then(before, after)
+    def between(k, place):
+        for (step, at_place), pairs in plan.items():
+            if at_place == place:
+
+                @pl.when(k == step)
+                def _():
+                    for before, after in pairs:
+                        then(before, after)
 
     factor_steps(work, between)
-    then(b_on, swaps[1])
+    for i in range(STEPS):
+        block = slice(i * TILE, (i + 1) * TILE)
+        xh_ref[block], xl_ref[block] = split2(work[block, PIVOTS:])
+    for copies in (top_first, top_last, bottom_first, bottom_last):
+        if copies in (top_last, bottom_last):
+            finish(copies)
+        ex.drain(copies)
+    solve_rows(lax.axis_size("row"), r, xh_ref, xl_ref, wrow_ref, uh_ref, ul_ref)
+    deliver(wrow_ref, solved_out)
+    deliver(uh_ref, uh_out)
+    deliver(ul_ref, ul_out)
     then(c_on, swaps[2])
-    for copies in (top_last, bottom_last, *swaps):
-        finish(copies)
+    bh_ref[:, :TILE] = jnp.zeros((PIVOTS, TILE), bf16)
+    bl_ref[:, :TILE] = jnp.zeros((PIVOTS, TILE), bf16)
+    for n in range(3):
+        finish(swaps[n])
+        first, last = TILE + n * 5 * TILE, TILE + (n + 1) * 5 * TILE
+        solve_cols(slice(first, last), xh_ref, xl_ref, wcol_ref, bh_ref, bl_ref)
+        done = pl.ds(first, last - first) if n else pl.ds(0, last)
+        deliver(bh_ref.at[:, done], bh_out.at[:, done])
+        deliver(bl_ref.at[:, done], bl_out.at[:, done])
     ex.drain()
-    for i in range(STEPS):
-        rows = slice(i * TILE, (i + 1) * TILE)
-        xh_ref[rows], xl_ref[rows] = split2(work[rows, PIVOTS:])
+    for copy in results:
+        copy.wait()
+
+
+def dot3(ah, al, bh, bl, dims):
+    def dot(p, q):
+        return lax.dot_general(p, q, (dims, ((), ())), preferred_element_type=f32)
+
+    return dot(ah, bh) + (dot(ah, bl) + dot(al, bh))
+
+
+QUARTER = 256
+
+
+def solve_rows(rows, r, xh_ref, xl_ref, wrow_ref, uh_ref, ul_ref):
+    @pl.loop(0, wrow_ref.shape[0] // QUARTER)
+    def _(i):
+        block = pl.ds(pl.multiple_of(i * QUARTER, QUARTER), QUARTER)
+        wh, wl = split2(wrow_ref[block, :])
+        slot = lax.broadcasted_iota(jnp.int32, (QUARTER, QUARTER), 0) // TILE + i * (QUARTER // TILE)
+        pivot = slot * rows + r < STEPS
+        for n in range(PIVOTS // QUARTER):
+            part = slice(n * QUARTER, (n + 1) * QUARTER)
+            depth = slice(0, (n + 1) * QUARTER)
+            b = dot3(wh[:, depth], wl[:, depth], xh_ref[part, depth], xl_ref[part, depth], ((1,), (1,)))
+            wrow_ref[block, part] = b
+            uh_ref[block, part], ul_ref[block, part] = split2(jnp.where(pivot, 0.0, b))
+
+
+def solve_cols(chunk, xh_ref, xl_ref, wcol_ref, bh_ref, bl_ref):
+    wh, wl = split2(wcol_ref[:, :, chunk].reshape(PIVOTS, chunk.stop - chunk.start))
+    for n in range(PIVOTS // QUARTER):
+        part = slice(n * QUARTER, (n + 1) * QUARTER)
+        depth = slice(0, (n + 1) * QUARTER)
+        b = dot3(xh_ref[part, depth], xl_ref[part, depth], wh[depth], wl[depth], ((1,), (0,)))
+        bh_ref[part, chunk], bl_ref[part, chunk] = split2(b)
 
 
 ROW_SPLIT = 768
@@ -484,96 +558,67 @@
 COPIES = 80
 
 
-def gather_and_factor(child_map, row_strip, col_strip, children):
+def gather_and_factor(child_map, front, children):
     vmem = pl.BlockSpec(memory_space=pltpu.VMEM)
-    local_rows, local_cols = row_strip.shape[0], col_strip.shape[1]
-    half = jax.ShapeDtypeStruct((PIVOTS, PIVOTS), bf16)
+    local_rows, local_cols = front.shape
     slices = (lax.axis_size("row") * lax.axis_size("col"), SUB, children.shape[2])
+    row_half = jax.ShapeDtypeStruct((local_rows, PIVOTS), bf16)
+    col_half = jax.ShapeDtypeStruct((PIVOTS, local_cols), bf16)
     return pl.pallas_call(
         gather_kernel,
         out_shape=(
-            half,
-            half,
             jax.ShapeDtypeStruct((local_rows, PIVOTS), f32),
-            jax.ShapeDtypeStruct((STEPS, TILE, local_cols), f32),
+            row_half,
+            row_half,
+            col_half,
+            col_half,
             jax.ShapeDtypeStruct(children.shape, f32),
         ),
-        in_specs=[pl.BlockSpec(memory_space=pltpu.SMEM)] + [vmem] * 3,
-        out_specs=(vmem,) * 5,
+        in_specs=[pl.BlockSpec(memory_space=pltpu.SMEM), pl.BlockSpec(memory_space=pl.ANY), vmem],
+        out_specs=(pl.BlockSpec(memory_space=pl.ANY),) * 6,
         scratch_shapes=[
+            pltpu.VMEM((local_rows, PIVOTS), f32),
+            pltpu.VMEM(row_half.shape, bf16),
+            pltpu.VMEM(row_half.shape, bf16),
+            pltpu.VMEM(col_half.shape, bf16),
+            pltpu.VMEM(col_half.shape, bf16),
+            pltpu.VMEM(children.shape, f32),
+            pltpu.VMEM((local_rows, TILE), f32),
+            pltpu.VMEM((TILE, local_cols), f32),
+            pltpu.VMEM((PIVOTS, PIVOTS), bf16),
+            pltpu.VMEM((PIVOTS, PIVOTS), bf16),
+            pltpu.VMEM((STEPS, TILE, local_cols), f32),
             pltpu.VMEM(slices, f32),
             pltpu.VMEM(slices, f32),
             pltpu.VMEM((2, 2, 4, 4, TILE, TILE), f32),
             pltpu.VMEM((PIVOTS, 2 * PIVOTS), f32),
+            pltpu.SemaphoreType.DMA((2,)),
+            pltpu.SemaphoreType.DMA((10,)),
             pltpu.SemaphoreType.DMA((4,)),
             pltpu.SemaphoreType.DMA((COPIES,)),
             pltpu.SemaphoreType.DMA((COPIES,)),
         ],
         compiler_params=pltpu.CompilerParams(
-            vmem_limit_bytes=56 * MIB, collective_id=0, has_side_effects=True
+            vmem_limit_bytes=60 * MIB, collective_id=0, has_side_effects=True
         ),
         cost_estimate=pl.CostEstimate(flops=5 * 10**10, bytes_accessed=8 * MIB, transcendentals=0),
         name="gather_factor",
-    )(child_map, row_strip, col_strip, children)
-
-
-def dot3(ah, al, bh, bl, dims):
-    def dot(p, q):
-        return lax.dot_general(p, q, (dims, ((), ())), preferred_element_type=f32)
-
-    return dot(ah, bh) + (dot(ah, bl) + dot(al, bh))
-
-
-QUARTER = 256
-
-
-def solve_rows_kernel(place_ref, w_ref, xh_ref, xl_ref, lower_ref, uh_ref, ul_ref):
+    )(child_map, front, children)
+
+
+def update_kernel(slots_ref, front_ref, moved_ref, solved_ref, uh_ref, ul_ref, bh_ref, bl_ref, out_ref, lower_ref):
     step = pl.program_id(0)
-    wh, wl = split2(w_ref[...])
-    count = w_ref.shape[0]
-    for n in range(PIVOTS // QUARTER):
-        block = slice(n * QUARTER, (n + 1) * QUARTER)
-        depth = slice(0, (n + 1) * QUARTER)
-        b = dot3(wh[:, depth], wl[:, depth], xh_ref[block, depth], xl_ref[block, depth], ((1,), (1,)))
-        row = lax.broadcasted_iota(jnp.int32, b.shape, 0)
-        row = row % TILE + (row // TILE + step * (count // TILE)) * (TILE * place_ref[0]) + place_ref[1] * TILE
-        col = lax.broadcasted_iota(jnp.int32, b.shape, 1) + n * QUARTER
-        lower_ref[:, block] = jnp.where(row >= col, b, 0.0)
-        uh_ref[:, block], ul_ref[:, block] = split2(jnp.where(row < PIVOTS, 0.0, b))
-
-
-def solve_rows(place, panel, xh, xl):
-    rows = panel.shape[0]
-    whole = pl.BlockSpec((PIVOTS, PIVOTS), lambda i: (0, 0))
-    block = pl.BlockSpec((QUARTER, PIVOTS), lambda i: (i, 0))
-    half = jax.ShapeDtypeStruct((rows, PIVOTS), bf16)
-    return pl.pallas_call(
-        solve_rows_kernel,
-        grid=(rows // QUARTER,),
-        out_shape=(jax.ShapeDtypeStruct((rows, PIVOTS), f32), half, half),
-        in_specs=[pl.BlockSpec(memory_space=pltpu.SMEM), block, whole, whole],
-        out_specs=(block,) * 3,
-        compiler_params=pltpu.CompilerParams(vmem_limit_bytes=40 * MIB),
-        name="solve_rows",
-    )(place, panel, xh, xl)
-
-
-def update_kernel(slots_ref, front_ref, moved_ref, w_ref, xh_ref, xl_ref, uh_ref, ul_ref, out_ref, bh, bl):
-    wh, wl = split2(w_ref[...].reshape(PIVOTS, QUARTER))
-    for n in range(PIVOTS // QUARTER):
-        block = slice(n * QUARTER, (n + 1) * QUARTER)
-        depth = slice(0, (n + 1) * QUARTER)
-        b = dot3(xh_ref[block, depth], xl_ref[block, depth], wh[depth], wl[depth], ((1,), (0,)))
-        col = lax.broadcasted_iota(jnp.int32, b.shape, 1) + pl.program_id(0) * QUARTER
-        bh[block], bl[block] = split2(jnp.where(col < TILE, 0.0, b))
+    row = lax.broadcasted_iota(jnp.int32, solved_ref.shape, 0) + slots_ref[2, step] * TILE
+    col = lax.broadcasted_iota(jnp.int32, solved_ref.shape, 1)
+    lower_ref[...] = jnp.where(row >= col, solved_ref[...], 0.0)
     for n in range(front_ref.shape[0] // QUARTER):
         block = slice(n * QUARTER, (n + 1) * QUARTER)
-        out_ref[block] = front_ref[block] - dot3(uh_ref[block], ul_ref[block], bh[...], bl[...], ((1,), (0,)))
+        out_ref[block] = front_ref[block] - dot3(uh_ref[block], ul_ref[block], bh_ref[...], bl_ref[...], ((1,), (0,)))
     for child in range(2):
         for tile in range(6):
             slot = slots_ref[1, child * 6 + tile]
 
-            @pl.when(slot // (QUARTER // TILE) == pl.program_id(0))
+            @pl.when(slot // (QUARTER // TILE) == step)
             def _():
                 col = pl.ds(pl.multiple_of(slot % (QUARTER // TILE) * TILE, TILE), TILE)
                 for run in range(3):
@@ -581,45 +626,43 @@
                     out_ref[row, col] += moved_ref[child, run * TILE : (run + 1) * TILE, tile * TILE : (tile + 1) * TILE]
 
 
-def update(slots, front, moved, panel, xh, xl, uh, ul):
+def update(slots, front, moved, solved, uh, ul, bh, bl):
     rows, cols = front.shape
-    whole = pl.BlockSpec((PIVOTS, PIVOTS), lambda j: (0, 0))
-    rows_whole = pl.BlockSpec((rows, PIVOTS), lambda j: (0, 0))
+    rows_whole = pl.BlockSpec((rows, PIVOTS), lambda j: (0, 0), pipeline_mode=pl.Buffered(1))
     block = pl.BlockSpec((rows, QUARTER), lambda j: (0, j))
+    cols_block = pl.BlockSpec((PIVOTS, QUARTER), lambda j: (0, j))
+    lower_block = pl.BlockSpec((rows // (cols // QUARTER), PIVOTS), lambda j: (j, 0))
     return pl.pallas_call(
         update_kernel,
         grid=(cols // QUARTER,),
-        out_shape=jax.ShapeDtypeStruct(front.shape, f32),
+        out_shape=(jax.ShapeDtypeStruct(front.shape, f32), jax.ShapeDtypeStruct(solved.shape, f32)),
         in_specs=[
             pl.BlockSpec(memory_space=pltpu.SMEM),
             block,
-            pl.BlockSpec(moved.shape, lambda j: (0, 0, 0)),
-            pl.BlockSpec((STEPS, TILE, QUARTER), lambda j: (0, 0, j)),
-            whole,
-            whole,
+            pl.BlockSpec(moved.shape, lambda j: (0, 0, 0), pipeline_mode=pl.Buffered(1)),
+            lower_block,
             rows_whole,
             rows_whole,
+            cols_block,
+            cols_block,
         ],
-        out_specs=block,
-        scratch_shapes=[pltpu.VMEM((PIVOTS, QUARTER), bf16)] * 2,
-        compiler_params=pltpu.CompilerParams(vmem_limit_bytes=40 * MIB),
+        out_specs=(block, lower_block),
+        compiler_params=pltpu.CompilerParams(vmem_limit_bytes=60 * MIB),
         name="update",
-    )(slots, front, moved, panel, xh, xl, uh, ul)
+    )(slots, front, moved, solved, uh, ul, bh, bl)
 
 
 def per_device(front, children, child_map):
     rows, cols = lax.axis_size("row"), lax.axis_size("col")
     row_index, col_index = lax.axis_index("row"), lax.axis_index("col")
-    xh, xl, row_panel, col_panel, moved = gather_and_factor(child_map, front[:, :TILE], front[:TILE, :], children)
-    place = jnp.stack([jnp.int32(rows), row_index])
-    lower_panel, uh, ul = solve_rows(place, row_panel, xh, xl)
+    solved, uh, ul, bh, bl, moved = gather_and_factor(child_map, front, children)
     starts = child_map[:, ::RUN]
     row_slots = (starts + (row_index - starts) % rows) // rows
     col_slots = (starts + (col_index - starts) % cols) // cols
     col_slots = col_slots[:, :, None] + jnp.arange(RUN // cols)[None, None, :]
-    slots = jnp.zeros((2, 12), jnp.int32).at[0, :6].set(row_slots.reshape(-1)).at[1].set(col_slots.reshape(-1))
-    front_out = update(slots, front, moved, col_panel, xh, xl, uh, ul)
-    return front_out, lower_panel
+    slots = jnp.zeros((3, 12), jnp.int32).at[0, :6].set(row_slots.reshape(-1)).at[1].set(col_slots.reshape(-1))
+    slots = slots.at[2].set(jnp.arange(12) * rows + row_index)
+    return update(slots, front, moved, solved, uh, ul, bh, bl)
 
 
 def solution(mesh):

time: 239 us -> 211 us (0.88)
  Pallas kernels: 228 us -> 209 us
  local copies, waits for them, and re-layouts: 10.5 us -> 1.01 us
    pallas_call x3 -> x2, Pallas kernels: 228 us -> 209 us  [the longest x1 187 us: gather_and_factor(): pl.pallas_call(gather_kernel, out_shape=(jax.ShapeDtypeStruct((local_rows...]
    unnamed x8 -> x2, local copies, waits for them, and re-layouts: 5.37 us -> 0.01 us
    slice x2 -> x0, local copies, waits for them, and re-layouts: 4.17 us -> none  [the longest x1 2.29 us: per_device(): front[:TILE, :]]
where the time goes in v4:
time: 211 us
  Pallas kernels  209 us (99%)
    pallas_call x1, Pallas kernels, gather_and_factor(): pl.pallas_call(gather_kernel, out_shape=(jax.ShapeDtypeStruct((local_rows...  187 us
    pallas_call x1, Pallas kernels, update(): pl.pallas_call(update_kernel, grid=(cols // QUARTER,), out_shape=(jax.Sha...  22.3 us

profile of v4, /device:TPU:7, one launch (start us, length us, event | category | flops | bytes accessed | tf_op | source)
XLA Modules:
  0.0 210.8 jit_solution(3930363394846932399)
XLA Ops:
  0.6 0.8 slice.49
  1.4 0.1 reshape.113
  1.5 0.1 iota_add_fusion
  1.6 0.1 add.67
  1.8 0.0 copy-start
  1.8 186.7 %gather_factor.1 = (f32[1024,1024]{1,0:T(8,128)}, bf16[1024,1024]{1,0:T(8,128)(2,1)}, bf16[1024,1024]{1,0:T(8,128)(2,1)}, bf16[1024,2048]{1,0:T(8,128)(2,1)}, bf...) custom-call(s32[2,48]{1,0:T(2,128)} %map_ref.1, f32[1024,2048]{1,0:T(8,128)} %front_ref.3, f32[2,384,768]{2,1,0:T(8,128)} %child_ref.1), custom_call_target="tpu_custom_call" | custom-call | flops 49999998976 | bytes 8388608 | tf_op jit(solution)/shard_map/gather_factor/pallas_call | solution.py:567
  188.5 0.0 copy-done
  188.5 22.3 %update.1 = (f32[1024,2048]{1,0:T(8,128)}, f32[1024,1024]{1,0:T(8,128)}) custom-call(s32[3,12]{1,0:T(4,128)} %copy-done, f32[1024,2048]{1,0:T(8,128)} %front_ref.3, f32[2,384,768]{2,1,0:T(8,128)} %get-tuple-element.44.moved_ref, f32[1024,1024]{1,0:T(8,128)} %get-tuple-element.45.solved_ref, bf16[1024,1024]{1,0:T(8,128)(2,1)} %get-tuple-element.46.uh_ref, ...), custom_call_target="tpu_custom_call" | custom-call | tf_op jit(solution)/shard_map/update/pallas_call | solution.py:635
  (5 shorter events, 0.1 us)
Async XLA Ops:
  1.8 186.7 %copy-start = (s32[3,12]{1,0:T(4,128)}, s32[3,12]{1,0:T(4,128)S(1)}, u32[]{:S(2)}) copy-start(s32[3,12]{1,0:T(4,128)S(1)} %scatter.14.slots_ref) | copy-start | bytes 436

commit v5 on v4

--- a/solution.py
+++ b/solution.py
@@ -30,14 +30,8 @@
     return hi, mid, rest - mid
 
 
-def mm3(a, b, dims):
-    ah, al = split2(a)
-    bh, bl = split2(b)
-
-    def dot(x, y):
-        return lax.dot_general(x, y, (dims, ((), ())), preferred_element_type=f32)
-
-    return dot(ah, bh) + (dot(ah, bl) + dot(al, bh))
+def stacked_dot(a, b, dim):
+    return lax.dot_general(a, b, (((dim,), (0,)), ((), ())), preferred_element_type=f32)
 
 
 def lane(x, k):
@@ -113,7 +107,7 @@
         work[i * TILE : (i + 1) * TILE, PIVOTS:] = (ri == ci).astype(f32)
 
 
-def factor_steps(work, between):
+def factor_steps(work, left_ref, right_ref, between):
     width = (STEPS + 1) * TILE
 
     @pl.loop(0, STEPS)
@@ -128,12 +122,20 @@
         e = [(ri + SUB * i == ci).astype(f32) for i in range(GROUPS)]
         inverse = factor_tile(a, e)
         between(k, 1)
-        work[kb, window] = mm3(inverse, work[kb, window], ((1,), (0,)))
+        lh, ll = split2(inverse)
+        wh, wl = split2(work[kb, window])
+        solved = stacked_dot(jnp.concatenate([lh, lh, ll], 1), jnp.concatenate([wh, wl, wh], 0), 1)
+        work[kb, window] = solved
+        ph, pl_ = split2(solved)
+        for n, (a_part, b_part) in enumerate(((ph, ph), (ph, pl_), (pl_, ph))):
+            left_ref[n * TILE : (n + 1) * TILE] = a_part
+            right_ref[n * TILE : (n + 1) * TILE] = b_part
 
         @pl.loop(k + 1, STEPS)
         def _(i):
             ib = pl.ds(pl.multiple_of(i * TILE, TILE), TILE)
-            work[ib, window] -= mm3(work[kb, ib], work[kb, window], ((0,), (0,)))
+            own = pl.ds(pl.multiple_of((i - k) * TILE, TILE), TILE)
+            work[ib, window] -= stacked_dot(left_ref[:, own], right_ref[...], 0)
 
 
 class Exchange:
@@ -275,7 +277,7 @@
 def gather_kernel(
     map_ref, front_ref, child_ref, solved_out, uh_out, ul_out, bh_out, bl_out, moved_out,
     wrow_ref, uh_ref, ul_ref, bh_ref, bl_ref, moved_ref,
-    strip_ref, cols_ref, xh_ref, xl_ref, wcol_ref, held, turned, pivots, work,
+    strip_ref, cols_ref, xh_ref, xl_ref, wcol_ref, held, turned, pivots, work, left_ref, right_ref,
     strip_sems, out_sems, relay_sems, send_sems, recv_sems,
 ):
     rows, cols = lax.axis_size("row"), lax.axis_size("col")
@@ -492,7 +494,7 @@
                     for before, after in pairs:
                         then(before, after)
 
-    factor_steps(work, between)
+    factor_steps(work, left_ref, right_ref, between)
     for i in range(STEPS):
         block = slice(i * TILE, (i + 1) * TILE)
         xh_ref[block], xl_ref[block] = split2(work[block, PIVOTS:])
@@ -592,6 +594,8 @@
             pltpu.VMEM(slices, f32),
             pltpu.VMEM((2, 2, 4, 4, TILE, TILE), f32),
             pltpu.VMEM((PIVOTS, 2 * PIVOTS), f32),
+            pltpu.VMEM((3 * TILE, (STEPS + 1) * TILE), bf16),
+            pltpu.VMEM((3 * TILE, (STEPS + 1) * TILE), bf16),
             pltpu.SemaphoreType.DMA((2,)),
             pltpu.SemaphoreType.DMA((10,)),
             pltpu.SemaphoreType.DMA((4,)),

time: 211 us -> 211 us (level)
  no operation moved by 1% of the time
where the time goes in v5:
time: 211 us; the launch traced here: 210 us
  Pallas kernels  208 us (99%)
    pallas_call x1, Pallas kernels, gather_and_factor(): pl.pallas_call(gather_kernel, out_shape=(jax.ShapeDtypeStruct((local_rows...  186 us
    pallas_call x1, Pallas kernels, update(): pl.pallas_call(update_kernel, grid=(cols // QUARTER,), out_shape=(jax.Sha...  22.3 us

profile of v5, /device:TPU:7, one launch (start us, length us, event | category | flops | bytes accessed | tf_op | source)
XLA Modules:
  0.0 209.6 jit_solution(18036319347687512677)
XLA Ops:
  0.6 0.8 slice.49
  1.4 0.1 reshape.113
  1.5 0.1 iota_add_fusion
  1.6 0.1 add.67
  1.8 0.0 copy-start
  1.8 185.5 %gather_factor.1 = (f32[1024,1024]{1,0:T(8,128)}, bf16[1024,1024]{1,0:T(8,128)(2,1)}, bf16[1024,1024]{1,0:T(8,128)(2,1)}, bf16[1024,2048]{1,0:T(8,128)(2,1)}, bf...) custom-call(s32[2,48]{1,0:T(2,128)} %map_ref.1, f32[1024,2048]{1,0:T(8,128)} %front_ref.3, f32[2,384,768]{2,1,0:T(8,128)} %child_ref.1), custom_call_target="tpu_custom_call" | custom-call | flops 49999998976 | bytes 8388608 | tf_op jit(solution)/shard_map/gather_factor/pallas_call | solution.py:569
  187.3 0.0 copy-done
  187.3 22.3 %update.1 = (f32[1024,2048]{1,0:T(8,128)}, f32[1024,1024]{1,0:T(8,128)}) custom-call(s32[3,12]{1,0:T(4,128)} %copy-done, f32[1024,2048]{1,0:T(8,128)} %front_ref.3, f32[2,384,768]{2,1,0:T(8,128)} %get-tuple-element.44.moved_ref, f32[1024,1024]{1,0:T(8,128)} %get-tuple-element.45.solved_ref, bf16[1024,1024]{1,0:T(8,128)(2,1)} %get-tuple-element.46.uh_ref, ...), custom_call_target="tpu_custom_call" | custom-call | tf_op jit(solution)/shard_map/update/pallas_call | solution.py:639
  (5 shorter events, 0.1 us)
Async XLA Ops:
  1.8 185.5 %copy-start = (s32[3,12]{1,0:T(4,128)}, s32[3,12]{1,0:T(4,128)S(1)}, u32[]{:S(2)}) copy-start(s32[3,12]{1,0:T(4,128)S(1)} %scatter.14.slots_ref) | copy-start | bytes 436
